TPU v7x, 32 devices: a whole 2x2x4 slice. The times are simulated.
32 devices in a mesh: seq: 8 (over z, y), tp: 4 (over x, core).
Axes of the slice: x: 2, y: 2, z: 4, core: 2. Of those that a mesh axis runs over, the one named last changes fastest.
Arguments:
- query_rows: bfloat16 [4096, 2560], P(('seq', 'tp')), may hold values from -6 to 6
- key_rows: bfloat16 [4096, 512], P(('seq', 'tp')), may hold values from -6 to 6
- value_rows: bfloat16 [4096, 512], P(('seq', 'tp')), may hold values from -6 to 6
- out_grad: bfloat16 [4096, 2560], P(('seq', 'tp')), may hold values from -6 to 6
- doc_lengths: int32 [8], replicated, may hold values from 1 to 1024, as said below
Outputs:
- attended: bfloat16 [4096, 2560], P(('seq', 'tp'))
- query_grad: bfloat16 [4096, 2560], P(('seq', 'tp'))
- key_grad: bfloat16 [4096, 512], P(('seq', 'tp'))
- value_grad: bfloat16 [4096, 512], P(('seq', 'tp'))
Inputs may be any that keep to these rules, and one draw needn't show every extreme that they name: `doc_lengths`: 8 document lengths in token order that sum to 4096; exactly one of them is 1024, all others are shorter.
All inputs are finite; a program needn't handle non-finite values.
Results may differ from a plain program's by a relative error of at most 0.022.
Values may be sent and summed in bfloat16 or wider, within the bound.
A program may use at most 64 MiB of HBM per device.

v0:
```python
import math

import jax
import jax.numpy as jnp
from jax import lax
from jax.sharding import PartitionSpec as P

HD = 128
QH = 20
KVH = 4


def passed_along(value, axis, by):
    peers = lax.axis_size(axis)
    pairs = [(i, i + by) for i in range(peers) if 0 <= i + by < peers]
    return lax.ppermute(value, axis, pairs)


def passed_along_2(block, axis, distance):
    devices = range(lax.axis_size(axis))
    route = [((i - distance) % len(devices), i) for i in devices]
    return lax.ppermute(block, axis, route)


def placed(first_row, row_count, doc_ends):
    position = first_row + jnp.arange(row_count, dtype=jnp.int32)
    segment = jnp.sum((position[:, None] >= doc_ends[None, :]).astype(jnp.int32), axis=1)
    return (position, segment)


def allowed(query_pos, query_seg, key_pos, key_seg):
    return (
        (key_pos[None, :] <= query_pos[:, None])
        & (key_pos[None, :] >= 0)
        & (key_seg[None, :] == query_seg[:, None])
    )


def absorb(softmax_state, query_heads, key_block, value_block, visible, scaling):
    running, denominator, accumulated = softmax_state
    scores = (
        jnp.einsum("bkgd,tkd->bkgt", query_heads, key_block, preferred_element_type=jnp.float32)
        * scaling
    )
    spread = visible[:, None, None, :]
    scores = jnp.where(spread, scores, -1e30)
    newest = jnp.maximum(running, jnp.max(scores, axis=-1))
    weight = jnp.where(spread, jnp.exp(scores - newest[..., None]), 0.0)
    shrink = jnp.exp(running - newest)
    denominator = denominator * shrink + jnp.sum(weight, axis=-1)
    accumulated = accumulated * shrink[..., None] + jnp.einsum(
        "bkgt,tkd->bkgd",
        weight.astype(jnp.bfloat16),
        value_block,
        preferred_element_type=jnp.float32,
    )
    return (newest, denominator, accumulated)


def contrib(query_heads, grad_heads, log_total, row_dot, key_block, value_block, visible, scaling):
    scores = (
        jnp.einsum("bkgd,tkd->bkgt", query_heads, key_block, preferred_element_type=jnp.float32)
        * scaling
    )
    spread = visible[:, None, None, :]
    scores = jnp.where(spread, scores, -1e30)
    probability = jnp.where(spread, jnp.exp(scores - log_total[..., None]), 0.0)
    value_part = jnp.einsum(
        "bkgt,bkgd->tkd",
        probability.astype(jnp.bfloat16),
        grad_heads,
        preferred_element_type=jnp.float32,
    )
    grad_prob = jnp.einsum(
        "bkgd,tkd->bkgt", grad_heads, value_block, preferred_element_type=jnp.float32
    )
    grad_score = (probability * (grad_prob - row_dot[..., None])).astype(jnp.bfloat16)
    query_part = (
        jnp.einsum("bkgt,tkd->bkgd", grad_score, key_block, preferred_element_type=jnp.float32)
        * scaling
    )
    key_part = (
        jnp.einsum("bkgt,bkgd->tkd", grad_score, query_heads, preferred_element_type=jnp.float32)
        * scaling
    )
    return (query_part, key_part, value_part)


def per_device(query_rows, key_rows, value_rows, out_grad, doc_lengths):
    per_kv = QH // KVH
    scaling = HD ** (-0.5)
    query_here, key_here, value_here, grad_here = (
        lax.all_to_all(query_rows, "tp", split_axis=1, concat_axis=0, tiled=True),
        lax.all_to_all(key_rows, "tp", split_axis=1, concat_axis=0, tiled=True),
        lax.all_to_all(value_rows, "tp", split_axis=1, concat_axis=0, tiled=True),
        lax.all_to_all(out_grad, "tp", split_axis=1, concat_axis=0, tiled=True),
    )
    length = query_here.shape[0]
    kv_heads = key_here.shape[1] // HD
    query_heads = query_here.reshape(length, kv_heads, per_kv, HD)
    grad_heads = grad_here.reshape(length, kv_heads, per_kv, HD)
    seq_count = lax.axis_size("seq")
    position = lax.axis_index("seq")
    doc_ends = jnp.cumsum(doc_lengths)
    query_pos, query_seg = placed(position * length, length, doc_ends)
    span_rows = math.gcd(length, 512)

    def sweep_keys(softmax_state, key_piece, value_piece, first_row):

        def sweep_advance(block_index, current):
            offset = block_index * span_rows
            key_block = key_piece.reshape(span_rows, kv_heads, HD)
            value_block = value_piece.reshape(span_rows, kv_heads, HD)
            key_pos, key_seg = placed(first_row + offset, span_rows, doc_ends)
            visible = allowed(query_pos, query_seg, key_pos, key_seg)
            return lax.cond(
                jnp.any(visible),
                lambda carried: absorb(
                    carried, query_heads, key_block, value_block, visible, scaling
                ),
                lambda carried: carried,
                current,
            )

        return lax.fori_loop(0, length // span_rows, sweep_advance, softmax_state)

    initial = (
        jnp.full((length, kv_heads, per_kv), -1e30, jnp.float32),
        jnp.zeros((length, kv_heads, per_kv), jnp.float32),
        jnp.zeros((length, kv_heads, per_kv, HD), jnp.float32),
    )
    softmax_state = sweep_keys(initial, key_here, value_here, position * length)

    def travel(turn_index, carried):
        current, key_value = carried
        key_value = passed_along(key_value, "seq", 1)
        current = sweep_keys(current, key_value[0], key_value[1], (position - turn_index) * length)
        return (current, key_value)

    softmax_state, spent = lax.fori_loop(
        1, seq_count, travel, (softmax_state, jnp.stack((key_here, value_here)))
    )
    running, denominator, accumulated = softmax_state
    out_heads = (accumulated / denominator[..., None]).astype(jnp.bfloat16)
    log_total = running + jnp.log(denominator)
    row_dot = jnp.sum(grad_heads.astype(jnp.float32) * out_heads.astype(jnp.float32), axis=-1)

    def backward_turn(turn_index, carried):
        query_acc, key_value, grad_sums = carried
        source_shard = (position - turn_index) % seq_count

        def backward_advance(block_index, inner_carry):
            query_inner, sums_inner = inner_carry
            offset = block_index * span_rows
            key_block = key_value[0].reshape(span_rows, kv_heads, HD)
            value_block = key_value[1].reshape(span_rows, kv_heads, HD)
            key_pos, key_seg = placed(source_shard * length + offset, span_rows, doc_ends)
            visible = allowed(query_pos, query_seg, key_pos, key_seg)

            def compute(unused):
                query_part, key_part, value_part = contrib(
                    query_heads,
                    grad_heads,
                    log_total,
                    row_dot,
                    key_block,
                    value_block,
                    visible,
                    scaling,
                )
                return (
                    query_part,
                    jnp.stack((key_part.reshape(span_rows, -1), value_part.reshape(span_rows, -1))),
                )

            def nothing(unused):
                return (
                    jnp.zeros_like(query_inner),
                    jnp.zeros((2, span_rows, key_value.shape[2]), jnp.float32),
                )

            query_part, key_value_part = lax.cond(jnp.any(visible), compute, nothing, 0)
            current = sums_inner
            sums_inner = current + key_value_part
            return (query_inner + query_part, sums_inner)

        query_acc, grad_sums = lax.fori_loop(
            0, length // span_rows, backward_advance, (query_acc, grad_sums)
        )
        key_value = passed_along(key_value, "seq", 1)
        grad_sums = passed_along_2(grad_sums.astype(jnp.bfloat16), "seq", 1).astype(grad_sums.dtype)
        return (query_acc, key_value, grad_sums)

    key_value = jnp.stack((key_here, value_here))
    start_sums = jnp.zeros(key_value.shape, jnp.float32)
    start_query = jnp.zeros((length, kv_heads, per_kv, HD), jnp.float32)
    query_acc, spent_pair, grad_sums = lax.fori_loop(
        0, seq_count, backward_turn, (start_query, key_value, start_sums)
    )
    outputs = (
        lax.all_to_all(
            out_heads.reshape(length, -1), "tp", split_axis=0, concat_axis=1, tiled=True
        ),
        lax.all_to_all(
            query_acc.astype(jnp.bfloat16).reshape(length, -1),
            "tp",
            split_axis=0,
            concat_axis=1,
            tiled=True,
        ),
        lax.all_to_all(
            grad_sums[0].astype(jnp.bfloat16), "tp", split_axis=0, concat_axis=1, tiled=True
        ),
        lax.all_to_all(
            grad_sums[1].astype(jnp.bfloat16), "tp", split_axis=0, concat_axis=1, tiled=True
        ),
    )
    return (outputs[0], outputs[1], outputs[2], outputs[3])


def solution(mesh):
    return jax.shard_map(
        per_device,
        mesh=mesh,
        in_specs=(
            P(("seq", "tp"), None),
            P(("seq", "tp"), None),
            P(("seq", "tp"), None),
            P(("seq", "tp"), None),
            P(),
        ),
        out_specs=(
            P(("seq", "tp"), None),
            P(("seq", "tp"), None),
            P(("seq", "tp"), None),
            P(("seq", "tp"), None),
        ),
        check_vma=False,
    )
```

profile of v0, /device:TPU:13, one launch (start us, length us, event | category | flops | bytes accessed | tf_op | source)
XLA Modules:
  0.0 329.1 jit_solution(6087948204931035635)
XLA Ops:
  2.3 4.0 %all-to-all-start = ((bf16[128,4,128]{0,2,1:T(8,128)(2,1)}), bf16[128,4,128]{0,2,1:T(8,128)(2,1)S(1)}, u32[]{:S(2)}, u32[]{:S(2)}) async-start(bf16[128,4,128]{0,2,1:T(8,128)(2,1)} %bitcast.59), calls=%async_computation | async-start | bytes 262144 | tf_op jit(solution)/shard_map/all_to_all | solution.py:94
  6.3 2.2 copy.108
  10.1 4.1 %all-to-all-start.2 = ((bf16[128,4,128]{0,2,1:T(8,128)(2,1)}), bf16[128,4,128]{0,2,1:T(8,128)(2,1)S(1)}, u32[]{:S(2)}, u32[]{:S(2)}) async-start(bf16[128,4,128]{0,2,1:T(8,128)(2,1)} %bitcast.63), calls=%async_computation.2 | async-start | bytes 262144 | tf_op jit(solution)/shard_map/all_to_all | solution.py:95
  14.2 3.6 %all-to-all-done.2 = bf16[128,4,128]{0,2,1:T(8,128)(2,1)S(1)} async-done(((bf16[128,4,128]{0,2,1:T(8,128)(2,1)}), bf16[128,4,128]{0,2,1:T(8,128)(2,1)S(1)}, u32[]{:S(2)}, u32[]{:S(2)}) %all-to-all-start.2) | async-done | bytes 131104 | tf_op jit(solution)/shard_map/all_to_all | solution.py:95
  17.8 4.5 %all-to-all-start.1 = ((bf16[128,4,640]{0,2,1:T(8,128)(2,1)}), bf16[128,4,640]{0,2,1:T(8,128)(2,1)S(1)}, u32[]{:S(2)}, u32[]{:S(2)}) async-start(bf16[128,4,640]{0,2,1:T(8,128)(2,1)} %bitcast.61), calls=%async_computation.1 | async-start | bytes 1310720 | tf_op jit(solution)/shard_map/all_to_all | solution.py:93
  24.9 1.8 compare_and_fusion.2
  27.4 2.2 copy.119
  31.7 5.0 %all-to-all-start.4 = ((bf16[128,4,640]{0,2,1:T(8,128)(2,1)}), bf16[128,4,640]{0,2,1:T(8,128)(2,1)}, u32[]{:S(2)}, u32[]{:S(2)}) async-start(bf16[128,4,640]{0,2,1:T(8,128)(2,1)} %bitcast.70), calls=%async_computation.4 | async-start | bytes 1310720 | tf_op jit(solution)/shard_map/all_to_all | solution.py:96
  37.8 10.6 %conditional.3 = ((f32[512,1,5]{0,2,1:T(8,128)S(1)}, f32[512,1,5]{0,2,1:T(8,128)S(1)}, f32[512,1,5,128]{3,0,2,1:T(8,128)})) conditional(s32[]{:T(128)} %convert_element_type.110, (f32[512,1,5]{0,2,1:T(8,128)S(1)}, f32[512,1,5]{0,2,1:T(8,128)S(1)}, f32[512,1,5,128]{3,0,2,1:T(8,128)}) %tuple.76, (pred[512,512]{0,1:T(8,128)(4,1)S(1)}, ...), branch_computations={%region_3.4_spmd, %region_4.7_spmd} | conditional | flops 688791040 | bytes 41713724 | solution.py:116
  39.0 2.3 copy-done
  42.7 5.7 %fusion.14 = f32[512,1,5,128]{3,0,2,1:T(8,128)} fusion(bf16[512,128,1]{1,0,2:T(8,128)(2,1)S(1)} %bitcast.265, f32[512,512,5]{1,0,2:T(8,128)} %copy-done, f32[512,5]{0,1:T(8,128)S(1)} %bitcast.264, pred[512,512]{0,1:T(8,128)(4,1)S(1)} %get-tuple-element.660, f32[512,1,5,128]{3,0,2,1:T(8,128)} %get-tuple-element.664, f32[512,5]{0,1:T(8,128)S(1)} %get-tuple-element.1002), kind=kOutput, calls=%fused_computation.11 | convolution fusion | flops 342753280 | bytes 8278016 | tf_op jit(solution)/shard_map/while/body/eval_jaxpr/cond/branch_1_fun/bkgt,tkd->bkgd/dot_general | solution.py:51
  48.4 66.5 %while.74 = (s32[]{:T(128)}, f32[512,1,5]{0,2,1:T(8,128)S(1)}, f32[512,1,5]{0,2,1:T(8,128)S(1)}, f32[512,1,5,128]{3,0,2,1:T(8,128)}, bf16[2,512,128]{2,1,0:T(8,1...) while((s32[]{:T(128)}, f32[512,1,5]{0,2,1:T(8,128)S(1)}, ...), condition=%wide.region_14.15_spmd.clone, body=%wide.region_7.14_spmd.clone.sunk | while | flops 690115584 | bytes 22082896 | solution.py:140
  48.4 3.1 collective-permute-start
  54.6 3.5 %collective-permute-done = bf16[2,512,128]{2,1,0:T(8,128)(2,1)S(1)} collective-permute-done((bf16[2,512,128]{2,1,0:T(8,128)(2,1)S(1)}, bf16[2,512,128]{2,1,0:T(8,128)(2,1)S(1)}, u32[]{:S(2)}, u32[]{:S(2)}) %collective-permute-start) | collective-permute-done | bytes 262176 | tf_op jit(solution)/shard_map/while/body/eval_jaxpr/ppermute | solution.py:16
  58.2 6.2 %conditional.8 = ((f32[512,1,5]{0,2,1:T(8,128)S(1)}, f32[512,1,5]{0,2,1:T(8,128)S(1)}, f32[512,1,5,128]{3,0,2,1:T(8,128)})) conditional(s32[]{:T(128)} %convert_element_type.163, (f32[512,1,5]{0,2,1:T(8,128)S(1)}, f32[512,1,5]{0,2,1:T(8,128)S(1)}, f32[512,1,5,128]{3,0,2,1:T(8,128)}) %tuple.142, (pred[512,512]{0,1:T(8,128)(4,1)S(1)}, ...), branch_computations={%region_10.10_spmd, %region_11.13_spmd} | conditional | flops 688791040 | bytes 20230176 | solution.py:116
  59.2 3.9 %fusion.33 = f32[512,1,5,128]{3,0,2,1:T(8,128)} fusion(f32[512,512,5]{1,0,2:T(8,128)S(1)} %get-tuple-element.1015, f32[512,5]{0,1:T(8,128)S(1)} %bitcast.247, pred[512,512]{0,1:T(8,128)(4,1)S(1)} %get-tuple-element.667, f32[512,1,5,128]{3,0,2,1:T(8,128)} %get-tuple-element.671, f32[512,5]{0,1:T(8,128)S(1)} %get-tuple-element.1004, ...), kind=kOutput, calls=%fused_computation.30 | convolution fusion | flops 342753280 | bytes 8290304 | tf_op jit(solution)/shard_map/while/body/eval_jaxpr/while/body/eval_jaxpr/cond/branch_1_fun/bkgt,tkd->bkgd/dot_general | solution.py:51
  64.4 4.1 %collective-permute-start = (bf16[2,512,128]{2,1,0:T(8,128)(2,1)S(1)}, bf16[2,512,128]{2,1,0:T(8,128)(2,1)S(1)}, u32[]{:S(2)}, u32[]{:S(2)}) collective-permute-start(bf16[2,512,128]{2,1,0:T(8,128)(2,1)S(1)} %get-tuple-element.1204), channel_id=1, source_target_pairs={{0,4},{4,8},{8,12},{12,16},{16,20},{20,24},{24,28},{1,5},{5,9},{9,... | collective-permute-start | bytes 786440 | tf_op jit(solution)/shard_map/while/body/eval_jaxpr/ppermute | solution.py:16
  73.3 5.0 %collective-permute-start = (bf16[2,512,128]{2,1,0:T(8,128)(2,1)S(1)}, bf16[2,512,128]{2,1,0:T(8,128)(2,1)S(1)}, u32[]{:S(2)}, u32[]{:S(2)}) collective-permute-start(bf16[2,512,128]{2,1,0:T(8,128)(2,1)S(1)} %get-tuple-element.1204), channel_id=1, source_target_pairs={{0,4},{4,8},{8,12},{12,16},{16,20},{20,24},{24,28},{1,5},{5,9},{9,... | collective-permute-start | bytes 786440 | tf_op jit(solution)/shard_map/while/body/eval_jaxpr/ppermute | solution.py:16
  82.2 5.0 %collective-permute-start = (bf16[2,512,128]{2,1,0:T(8,128)(2,1)S(1)}, bf16[2,512,128]{2,1,0:T(8,128)(2,1)S(1)}, u32[]{:S(2)}, u32[]{:S(2)}) collective-permute-start(bf16[2,512,128]{2,1,0:T(8,128)(2,1)S(1)} %get-tuple-element.1204), channel_id=1, source_target_pairs={{0,4},{4,8},{8,12},{12,16},{16,20},{20,24},{24,28},{1,5},{5,9},{9,... | collective-permute-start | bytes 786440 | tf_op jit(solution)/shard_map/while/body/eval_jaxpr/ppermute | solution.py:16
  90.6 4.7 %collective-permute-start = (bf16[2,512,128]{2,1,0:T(8,128)(2,1)S(1)}, bf16[2,512,128]{2,1,0:T(8,128)(2,1)S(1)}, u32[]{:S(2)}, u32[]{:S(2)}) collective-permute-start(bf16[2,512,128]{2,1,0:T(8,128)(2,1)S(1)} %get-tuple-element.1204), channel_id=1, source_target_pairs={{0,4},{4,8},{8,12},{12,16},{16,20},{20,24},{24,28},{1,5},{5,9},{9,... | collective-permute-start | bytes 786440 | tf_op jit(solution)/shard_map/while/body/eval_jaxpr/ppermute | solution.py:16
  98.6 4.7 %collective-permute-start = (bf16[2,512,128]{2,1,0:T(8,128)(2,1)S(1)}, bf16[2,512,128]{2,1,0:T(8,128)(2,1)S(1)}, u32[]{:S(2)}, u32[]{:S(2)}) collective-permute-start(bf16[2,512,128]{2,1,0:T(8,128)(2,1)S(1)} %get-tuple-element.1204), channel_id=1, source_target_pairs={{0,4},{4,8},{8,12},{12,16},{16,20},{20,24},{24,28},{1,5},{5,9},{9,... | collective-permute-start | bytes 786440 | tf_op jit(solution)/shard_map/while/body/eval_jaxpr/ppermute | solution.py:16
  106.7 4.7 %collective-permute-start = (bf16[2,512,128]{2,1,0:T(8,128)(2,1)S(1)}, bf16[2,512,128]{2,1,0:T(8,128)(2,1)S(1)}, u32[]{:S(2)}, u32[]{:S(2)}) collective-permute-start(bf16[2,512,128]{2,1,0:T(8,128)(2,1)S(1)} %get-tuple-element.1204), channel_id=1, source_target_pairs={{0,4},{4,8},{8,12},{12,16},{16,20},{20,24},{24,28},{1,5},{5,9},{9,... | collective-permute-start | bytes 786440 | tf_op jit(solution)/shard_map/while/body/eval_jaxpr/ppermute | solution.py:16
  116.6 2.4 copy.120
  124.0 142.8 %while.75 = (s32[]{:T(128)}, f32[512,1,5,128]{3,0,2,1:T(8,128)}, bf16[2,512,128]{2,1,0:T(8,128)(2,1)S(1)}, f32[2,512,128]{2,1,0:T(8,128)S(1)}, s32[]{:T(128)}, /...) while((s32[]{:T(128)}, f32[512,1,5,128]{3,0,2,1:T(8,128)}, ...), condition=%wide.region_21.22_spmd.clone, body=%wide.region_16.21_spmd.clone.sunk | while | flops 1696478720 | bytes 41610760 | solution.py:197
  124.7 4.7 %collective-permute-start.1 = (bf16[2,512,128]{2,1,0:T(8,128)(2,1)}, bf16[2,512,128]{2,1,0:T(8,128)(2,1)S(1)}, u32[]{:S(2)}, u32[]{:S(2)}) collective-permute-start(bf16[2,512,128]{2,1,0:T(8,128)(2,1)} %copy.171), channel_id=1, source_target_pairs={{0,4},{4,8},{8,12},{12,16},{16,20},{20,24},{24,28},{1,5},{5,9},{9,... | collective-permute-start | bytes 786440 | tf_op jit(solution)/shard_map/while/body/eval_jaxpr/ppermute | solution.py:16
  132.5 9.5 %conditional.9 = (f32[512,1,5,128]{3,0,2,1:T(8,128)S(1)}, f32[2,512,128]{2,1,0:T(8,128)S(1)}) conditional(s32[]{:T(128)} %convert_element_type.166, () %tuple.146, (pred[512,512]{0,1:T(8,128)(4,1)S(1)}, bf16[2,512,128]{2,1,0:T(8,128)(2,1)}, bf16[512,1,5,128]{3,0,2,1:T(8,128)(2,1)S(1)}, f32[512,1,5]{0,2,1:T(8,128)}, ...), branch_computations={%region_19.19_spmd, %region_20.20_spmd} | conditional | flops 1693974528 | bytes 32679980 | solution.py:182
  132.6 1.8 fusion.65
  134.4 2.8 fusion.52
  138.1 2.1 fusion.59
  140.3 1.8 fusion.56
  142.1 2.3 collective-permute-start.2
  145.7 2.1 collective-permute-done.2
  148.5 4.7 %collective-permute-start.1 = (bf16[2,512,128]{2,1,0:T(8,128)(2,1)}, bf16[2,512,128]{2,1,0:T(8,128)(2,1)S(1)}, u32[]{:S(2)}, u32[]{:S(2)}) collective-permute-start(bf16[2,512,128]{2,1,0:T(8,128)(2,1)} %copy.171), channel_id=1, source_target_pairs={{0,4},{4,8},{8,12},{12,16},{16,20},{20,24},{24,28},{1,5},{5,9},{9,... | collective-permute-start | bytes 786440 | tf_op jit(solution)/shard_map/while/body/eval_jaxpr/ppermute | solution.py:16
  156.3 9.5 %conditional.9 = (f32[512,1,5,128]{3,0,2,1:T(8,128)S(1)}, f32[2,512,128]{2,1,0:T(8,128)S(1)}) conditional(s32[]{:T(128)} %convert_element_type.166, () %tuple.146, (pred[512,512]{0,1:T(8,128)(4,1)S(1)}, bf16[2,512,128]{2,1,0:T(8,128)(2,1)}, bf16[512,1,5,128]{3,0,2,1:T(8,128)(2,1)S(1)}, f32[512,1,5]{0,2,1:T(8,128)}, ...), branch_computations={%region_19.19_spmd, %region_20.20_spmd} | conditional | flops 1693974528 | bytes 32679980 | solution.py:182
  156.4 1.8 fusion.65
  158.2 2.8 fusion.52
  161.9 2.1 fusion.59
  164.1 1.8 fusion.56
  166.0 2.0 collective-permute-start.2
  167.9 2.6 select_add_fusion.3
  172.0 4.7 %collective-permute-start.1 = (bf16[2,512,128]{2,1,0:T(8,128)(2,1)}, bf16[2,512,128]{2,1,0:T(8,128)(2,1)S(1)}, u32[]{:S(2)}, u32[]{:S(2)}) collective-permute-start(bf16[2,512,128]{2,1,0:T(8,128)(2,1)} %copy.171), channel_id=1, source_target_pairs={{0,4},{4,8},{8,12},{12,16},{16,20},{20,24},{24,28},{1,5},{5,9},{9,... | collective-permute-start | bytes 786440 | tf_op jit(solution)/shard_map/while/body/eval_jaxpr/ppermute | solution.py:16
  181.2 2.6 select_add_fusion.3
  183.7 2.3 collective-permute-done.2
  186.8 4.7 %collective-permute-start.1 = (bf16[2,512,128]{2,1,0:T(8,128)(2,1)}, bf16[2,512,128]{2,1,0:T(8,128)(2,1)S(1)}, u32[]{:S(2)}, u32[]{:S(2)}) collective-permute-start(bf16[2,512,128]{2,1,0:T(8,128)(2,1)} %copy.171), channel_id=1, source_target_pairs={{0,4},{4,8},{8,12},{12,16},{16,20},{20,24},{24,28},{1,5},{5,9},{9,... | collective-permute-start | bytes 786440 | tf_op jit(solution)/shard_map/while/body/eval_jaxpr/ppermute | solution.py:16
  195.0 2.6 select_add_fusion.3
  197.5 5.9 %collective-permute-done.2 = bf16[2,512,128]{2,1,0:T(8,128)(2,1)S(1)} collective-permute-done((bf16[2,512,128]{2,1,0:T(8,128)(2,1)S(1)}, bf16[2,512,128]{2,1,0:T(8,128)(2,1)S(1)}, u32[]{:S(2)}, u32[]{:S(2)}) %collective-permute-start.2) | collective-permute-done | bytes 262176 | tf_op jit(solution)/shard_map/while/body/eval_jaxpr/ppermute | solution.py:22
  204.2 4.8 %collective-permute-start.1 = (bf16[2,512,128]{2,1,0:T(8,128)(2,1)}, bf16[2,512,128]{2,1,0:T(8,128)(2,1)S(1)}, u32[]{:S(2)}, u32[]{:S(2)}) collective-permute-start(bf16[2,512,128]{2,1,0:T(8,128)(2,1)} %copy.171), channel_id=1, source_target_pairs={{0,4},{4,8},{8,12},{12,16},{16,20},{20,24},{24,28},{1,5},{5,9},{9,... | collective-permute-start | bytes 786440 | tf_op jit(solution)/shard_map/while/body/eval_jaxpr/ppermute | solution.py:16
  212.4 2.6 select_add_fusion.3
  215.0 5.1 %collective-permute-done.2 = bf16[2,512,128]{2,1,0:T(8,128)(2,1)S(1)} collective-permute-done((bf16[2,512,128]{2,1,0:T(8,128)(2,1)S(1)}, bf16[2,512,128]{2,1,0:T(8,128)(2,1)S(1)}, u32[]{:S(2)}, u32[]{:S(2)}) %collective-permute-start.2) | collective-permute-done | bytes 262176 | tf_op jit(solution)/shard_map/while/body/eval_jaxpr/ppermute | solution.py:22
  220.9 5.0 %collective-permute-start.1 = (bf16[2,512,128]{2,1,0:T(8,128)(2,1)}, bf16[2,512,128]{2,1,0:T(8,128)(2,1)S(1)}, u32[]{:S(2)}, u32[]{:S(2)}) collective-permute-start(bf16[2,512,128]{2,1,0:T(8,128)(2,1)} %copy.171), channel_id=1, source_target_pairs={{0,4},{4,8},{8,12},{12,16},{16,20},{20,24},{24,28},{1,5},{5,9},{9,... | collective-permute-start | bytes 786440 | tf_op jit(solution)/shard_map/while/body/eval_jaxpr/ppermute | solution.py:16
  229.3 2.6 select_add_fusion.3
  231.9 4.2 %collective-permute-done.2 = bf16[2,512,128]{2,1,0:T(8,128)(2,1)S(1)} collective-permute-done((bf16[2,512,128]{2,1,0:T(8,128)(2,1)S(1)}, bf16[2,512,128]{2,1,0:T(8,128)(2,1)S(1)}, u32[]{:S(2)}, u32[]{:S(2)}) %collective-permute-start.2) | collective-permute-done | bytes 262176 | tf_op jit(solution)/shard_map/while/body/eval_jaxpr/ppermute | solution.py:22
  236.8 5.0 %collective-permute-start.1 = (bf16[2,512,128]{2,1,0:T(8,128)(2,1)}, bf16[2,512,128]{2,1,0:T(8,128)(2,1)S(1)}, u32[]{:S(2)}, u32[]{:S(2)}) collective-permute-start(bf16[2,512,128]{2,1,0:T(8,128)(2,1)} %copy.171), channel_id=1, source_target_pairs={{0,4},{4,8},{8,12},{12,16},{16,20},{20,24},{24,28},{1,5},{5,9},{9,... | collective-permute-start | bytes 786440 | tf_op jit(solution)/shard_map/while/body/eval_jaxpr/ppermute | solution.py:16
  245.2 2.6 select_add_fusion.3
  247.8 3.5 %collective-permute-done.2 = bf16[2,512,128]{2,1,0:T(8,128)(2,1)S(1)} collective-permute-done((bf16[2,512,128]{2,1,0:T(8,128)(2,1)S(1)}, bf16[2,512,128]{2,1,0:T(8,128)(2,1)S(1)}, u32[]{:S(2)}, u32[]{:S(2)}) %collective-permute-start.2) | collective-permute-done | bytes 262176 | tf_op jit(solution)/shard_map/while/body/eval_jaxpr/ppermute | solution.py:22
  252.1 5.0 %collective-permute-start.1 = (bf16[2,512,128]{2,1,0:T(8,128)(2,1)}, bf16[2,512,128]{2,1,0:T(8,128)(2,1)S(1)}, u32[]{:S(2)}, u32[]{:S(2)}) collective-permute-start(bf16[2,512,128]{2,1,0:T(8,128)(2,1)} %copy.171), channel_id=1, source_target_pairs={{0,4},{4,8},{8,12},{12,16},{16,20},{20,24},{24,28},{1,5},{5,9},{9,... | collective-permute-start | bytes 786440 | tf_op jit(solution)/shard_map/while/body/eval_jaxpr/ppermute | solution.py:16
  260.6 2.6 select_add_fusion.3
  263.1 3.6 %collective-permute-done.2 = bf16[2,512,128]{2,1,0:T(8,128)(2,1)S(1)} collective-permute-done((bf16[2,512,128]{2,1,0:T(8,128)(2,1)S(1)}, bf16[2,512,128]{2,1,0:T(8,128)(2,1)S(1)}, u32[]{:S(2)}, u32[]{:S(2)}) %collective-permute-start.2) | collective-permute-done | bytes 262176 | tf_op jit(solution)/shard_map/while/body/eval_jaxpr/ppermute | solution.py:22
  267.5 25.0 %all_to_all.134 = bf16[4,128,128]{2,1,0:T(8,128)(2,1)S(1)} all-to-all(bf16[4,128,128]{2,1,0:T(8,128)(2,1)S(1)} %bitcast.260), channel_id=1, replica_groups=mesh['seq'=8,'tp'=4] {'tp'}, dimensions={0} | all-to-all | bytes 262144 | tf_op jit(solution)/shard_map/all_to_all | solution.py:211
  292.5 4.3 %all-to-all-start.7 = ((bf16[4,128,128]{2,1,0:T(8,128)(2,1)}), bf16[4,128,128]{2,1,0:T(8,128)(2,1)S(1)}, u32[]{:S(2)}, u32[]{:S(2)}) async-start(bf16[4,128,128]{2,1,0:T(8,128)(2,1)} %bitcast.78), calls=%async_computation.7 | async-start | bytes 262144 | tf_op jit(solution)/shard_map/all_to_all | solution.py:214
  300.4 4.5 %all-to-all-start.5 = ((bf16[4,128,640]{1,2,0:T(8,128)(2,1)}), bf16[4,128,640]{1,2,0:T(8,128)(2,1)S(1)}, u32[]{:S(2)}, u32[]{:S(2)}) async-start(bf16[4,128,640]{1,2,0:T(8,128)(2,1)} %copy.124), calls=%async_computation.5 | async-start | bytes 1310720 | tf_op jit(solution)/shard_map/all_to_all | solution.py:204
  306.0 8.3 %all-to-all-done.5 = bf16[4,128,640]{1,2,0:T(8,128)(2,1)S(1)} async-done(((bf16[4,128,640]{1,2,0:T(8,128)(2,1)}), bf16[4,128,640]{1,2,0:T(8,128)(2,1)S(1)}, u32[]{:S(2)}, u32[]{:S(2)}) %all-to-all-start.5) | async-done | bytes 655392 | tf_op jit(solution)/shard_map/all_to_all | solution.py:204
  314.3 4.3 %all-to-all-start.3 = ((bf16[4,128,640]{1,2,0:T(8,128)(2,1)}), bf16[4,128,640]{1,2,0:T(8,128)(2,1)S(1)}, u32[]{:S(2)}, u32[]{:S(2)}) async-start(bf16[4,128,640]{1,2,0:T(8,128)(2,1)} %copy.118), calls=%async_computation.3 | async-start | bytes 1310720 | tf_op jit(solution)/shard_map/all_to_all | solution.py:201
  321.5 6.5 %all-to-all-done.3 = bf16[4,128,640]{1,2,0:T(8,128)(2,1)S(1)} async-done(((bf16[4,128,640]{1,2,0:T(8,128)(2,1)}), bf16[4,128,640]{1,2,0:T(8,128)(2,1)S(1)}, u32[]{:S(2)}, u32[]{:S(2)}) %all-to-all-start.3) | async-done | bytes 655392 | tf_op jit(solution)/shard_map/all_to_all | solution.py:201
  (218 shorter events, 83.5 us)
Async XLA Ops:
  2.3 7.8 %all-to-all-start = ((bf16[128,4,128]{0,2,1:T(8,128)(2,1)}), bf16[128,4,128]{0,2,1:T(8,128)(2,1)S(1)}, u32[]{:S(2)}, u32[]{:S(2)}) async-start(bf16[128,4,128]{0,2,1:T(8,128)(2,1)} %bitcast.59), calls=%async_computation | async-start | bytes 262144 | tf_op jit(solution)/shard_map/all_to_all | solution.py:94
  10.1 7.7 %all-to-all-start.2 = ((bf16[128,4,128]{0,2,1:T(8,128)(2,1)}), bf16[128,4,128]{0,2,1:T(8,128)(2,1)S(1)}, u32[]{:S(2)}, u32[]{:S(2)}) async-start(bf16[128,4,128]{0,2,1:T(8,128)(2,1)} %bitcast.63), calls=%async_computation.2 | async-start | bytes 262144 | tf_op jit(solution)/shard_map/all_to_all | solution.py:95
  17.8 13.9 %all-to-all-start.1 = ((bf16[128,4,640]{0,2,1:T(8,128)(2,1)}), bf16[128,4,640]{0,2,1:T(8,128)(2,1)S(1)}, u32[]{:S(2)}, u32[]{:S(2)}) async-start(bf16[128,4,640]{0,2,1:T(8,128)(2,1)} %bitcast.61), calls=%async_computation.1 | async-start | bytes 1310720 | tf_op jit(solution)/shard_map/all_to_all | solution.py:93
  31.7 84.9 %all-to-all-start.4 = ((bf16[128,4,640]{0,2,1:T(8,128)(2,1)}), bf16[128,4,640]{0,2,1:T(8,128)(2,1)}, u32[]{:S(2)}, u32[]{:S(2)}) async-start(bf16[128,4,640]{0,2,1:T(8,128)(2,1)} %bitcast.70), calls=%async_computation.4 | async-start | bytes 1310720 | tf_op jit(solution)/shard_map/all_to_all | solution.py:96
  37.8 10.6 %copy-start.3 = (bf16[2,512,128]{2,1,0:T(8,128)(2,1)S(1)}, bf16[2,512,128]{2,1,0:T(8,128)(2,1)}, u32[]{:S(2)}) copy-start(bf16[2,512,128]{2,1,0:T(8,128)(2,1)} %copy.154) | copy-start | bytes 786436
  39.0 2.3 copy-start
  48.4 9.8 %collective-permute-start = (bf16[2,512,128]{2,1,0:T(8,128)(2,1)S(1)}, bf16[2,512,128]{2,1,0:T(8,128)(2,1)S(1)}, u32[]{:S(2)}, u32[]{:S(2)}) collective-permute-start(bf16[2,512,128]{2,1,0:T(8,128)(2,1)S(1)} %get-tuple-element.1204), channel_id=1, source_target_pairs={{0,4},{4,8},{8,12},{12,16},{16,20},{20,24},{24,28},{1,5},{5,9},{9,... | collective-permute-start | bytes 786440 | tf_op jit(solution)/shard_map/while/body/eval_jaxpr/ppermute | solution.py:16
  64.4 8.9 %collective-permute-start = (bf16[2,512,128]{2,1,0:T(8,128)(2,1)S(1)}, bf16[2,512,128]{2,1,0:T(8,128)(2,1)S(1)}, u32[]{:S(2)}, u32[]{:S(2)}) collective-permute-start(bf16[2,512,128]{2,1,0:T(8,128)(2,1)S(1)} %get-tuple-element.1204), channel_id=1, source_target_pairs={{0,4},{4,8},{8,12},{12,16},{16,20},{20,24},{24,28},{1,5},{5,9},{9,... | collective-permute-start | bytes 786440 | tf_op jit(solution)/shard_map/while/body/eval_jaxpr/ppermute | solution.py:16
  73.3 8.8 %collective-permute-start = (bf16[2,512,128]{2,1,0:T(8,128)(2,1)S(1)}, bf16[2,512,128]{2,1,0:T(8,128)(2,1)S(1)}, u32[]{:S(2)}, u32[]{:S(2)}) collective-permute-start(bf16[2,512,128]{2,1,0:T(8,128)(2,1)S(1)} %get-tuple-element.1204), channel_id=1, source_target_pairs={{0,4},{4,8},{8,12},{12,16},{16,20},{20,24},{24,28},{1,5},{5,9},{9,... | collective-permute-start | bytes 786440 | tf_op jit(solution)/shard_map/while/body/eval_jaxpr/ppermute | solution.py:16
  82.2 8.3 %collective-permute-start = (bf16[2,512,128]{2,1,0:T(8,128)(2,1)S(1)}, bf16[2,512,128]{2,1,0:T(8,128)(2,1)S(1)}, u32[]{:S(2)}, u32[]{:S(2)}) collective-permute-start(bf16[2,512,128]{2,1,0:T(8,128)(2,1)S(1)} %get-tuple-element.1204), channel_id=1, source_target_pairs={{0,4},{4,8},{8,12},{12,16},{16,20},{20,24},{24,28},{1,5},{5,9},{9,... | collective-permute-start | bytes 786440 | tf_op jit(solution)/shard_map/while/body/eval_jaxpr/ppermute | solution.py:16
  90.6 8.0 %collective-permute-start = (bf16[2,512,128]{2,1,0:T(8,128)(2,1)S(1)}, bf16[2,512,128]{2,1,0:T(8,128)(2,1)S(1)}, u32[]{:S(2)}, u32[]{:S(2)}) collective-permute-start(bf16[2,512,128]{2,1,0:T(8,128)(2,1)S(1)} %get-tuple-element.1204), channel_id=1, source_target_pairs={{0,4},{4,8},{8,12},{12,16},{16,20},{20,24},{24,28},{1,5},{5,9},{9,... | collective-permute-start | bytes 786440 | tf_op jit(solution)/shard_map/while/body/eval_jaxpr/ppermute | solution.py:16
  98.6 8.0 %collective-permute-start = (bf16[2,512,128]{2,1,0:T(8,128)(2,1)S(1)}, bf16[2,512,128]{2,1,0:T(8,128)(2,1)S(1)}, u32[]{:S(2)}, u32[]{:S(2)}) collective-permute-start(bf16[2,512,128]{2,1,0:T(8,128)(2,1)S(1)} %get-tuple-element.1204), channel_id=1, source_target_pairs={{0,4},{4,8},{8,12},{12,16},{16,20},{20,24},{24,28},{1,5},{5,9},{9,... | collective-permute-start | bytes 786440 | tf_op jit(solution)/shard_map/while/body/eval_jaxpr/ppermute | solution.py:16
  106.7 8.2 %collective-permute-start = (bf16[2,512,128]{2,1,0:T(8,128)(2,1)S(1)}, bf16[2,512,128]{2,1,0:T(8,128)(2,1)S(1)}, u32[]{:S(2)}, u32[]{:S(2)}) collective-permute-start(bf16[2,512,128]{2,1,0:T(8,128)(2,1)S(1)} %get-tuple-element.1204), channel_id=1, source_target_pairs={{0,4},{4,8},{8,12},{12,16},{16,20},{20,24},{24,28},{1,5},{5,9},{9,... | collective-permute-start | bytes 786440 | tf_op jit(solution)/shard_map/while/body/eval_jaxpr/ppermute | solution.py:16
  124.7 23.1 %collective-permute-start.1 = (bf16[2,512,128]{2,1,0:T(8,128)(2,1)}, bf16[2,512,128]{2,1,0:T(8,128)(2,1)S(1)}, u32[]{:S(2)}, u32[]{:S(2)}) collective-permute-start(bf16[2,512,128]{2,1,0:T(8,128)(2,1)} %copy.171), channel_id=1, source_target_pairs={{0,4},{4,8},{8,12},{12,16},{16,20},{20,24},{24,28},{1,5},{5,9},{9,... | collective-permute-start | bytes 786440 | tf_op jit(solution)/shard_map/while/body/eval_jaxpr/ppermute | solution.py:16
  132.5 1.8 copy-start.2
  142.1 5.6 %collective-permute-start.2 = (bf16[2,512,128]{2,1,0:T(8,128)(2,1)S(1)}, bf16[2,512,128]{2,1,0:T(8,128)(2,1)S(1)}, u32[]{:S(2)}, u32[]{:S(2)}) collective-permute-start(bf16[2,512,128]{2,1,0:T(8,128)(2,1)S(1)} %fusion.90), channel_id=1, source_target_pairs={{28,0},{0,4},{4,8},{8,12},{12,16},{16,20},{20,24},{24,28},{29,1},{... | collective-permute-start | bytes 786440 | tf_op jit(solution)/shard_map/while/body/eval_jaxpr/ppermute | solution.py:22
  148.5 22.8 %collective-permute-start.1 = (bf16[2,512,128]{2,1,0:T(8,128)(2,1)}, bf16[2,512,128]{2,1,0:T(8,128)(2,1)S(1)}, u32[]{:S(2)}, u32[]{:S(2)}) collective-permute-start(bf16[2,512,128]{2,1,0:T(8,128)(2,1)} %copy.171), channel_id=1, source_target_pairs={{0,4},{4,8},{8,12},{12,16},{16,20},{20,24},{24,28},{1,5},{5,9},{9,... | collective-permute-start | bytes 786440 | tf_op jit(solution)/shard_map/while/body/eval_jaxpr/ppermute | solution.py:16
  156.4 1.8 copy-start.2
  166.0 5.3 %collective-permute-start.2 = (bf16[2,512,128]{2,1,0:T(8,128)(2,1)S(1)}, bf16[2,512,128]{2,1,0:T(8,128)(2,1)S(1)}, u32[]{:S(2)}, u32[]{:S(2)}) collective-permute-start(bf16[2,512,128]{2,1,0:T(8,128)(2,1)S(1)} %fusion.90), channel_id=1, source_target_pairs={{28,0},{0,4},{4,8},{8,12},{12,16},{16,20},{20,24},{24,28},{29,1},{... | collective-permute-start | bytes 786440 | tf_op jit(solution)/shard_map/while/body/eval_jaxpr/ppermute | solution.py:22
  172.0 14.1 %collective-permute-start.1 = (bf16[2,512,128]{2,1,0:T(8,128)(2,1)}, bf16[2,512,128]{2,1,0:T(8,128)(2,1)S(1)}, u32[]{:S(2)}, u32[]{:S(2)}) collective-permute-start(bf16[2,512,128]{2,1,0:T(8,128)(2,1)} %copy.171), channel_id=1, source_target_pairs={{0,4},{4,8},{8,12},{12,16},{16,20},{20,24},{24,28},{1,5},{5,9},{9,... | collective-permute-start | bytes 786440 | tf_op jit(solution)/shard_map/while/body/eval_jaxpr/ppermute | solution.py:16
  180.1 6.0 %collective-permute-start.2 = (bf16[2,512,128]{2,1,0:T(8,128)(2,1)S(1)}, bf16[2,512,128]{2,1,0:T(8,128)(2,1)S(1)}, u32[]{:S(2)}, u32[]{:S(2)}) collective-permute-start(bf16[2,512,128]{2,1,0:T(8,128)(2,1)S(1)} %fusion.90), channel_id=1, source_target_pairs={{28,0},{0,4},{4,8},{8,12},{12,16},{16,20},{20,24},{24,28},{29,1},{... | collective-permute-start | bytes 786440 | tf_op jit(solution)/shard_map/while/body/eval_jaxpr/ppermute | solution.py:22
  186.8 16.6 %collective-permute-start.1 = (bf16[2,512,128]{2,1,0:T(8,128)(2,1)}, bf16[2,512,128]{2,1,0:T(8,128)(2,1)S(1)}, u32[]{:S(2)}, u32[]{:S(2)}) collective-permute-start(bf16[2,512,128]{2,1,0:T(8,128)(2,1)} %copy.171), channel_id=1, source_target_pairs={{0,4},{4,8},{8,12},{12,16},{16,20},{20,24},{24,28},{1,5},{5,9},{9,... | collective-permute-start | bytes 786440 | tf_op jit(solution)/shard_map/while/body/eval_jaxpr/ppermute | solution.py:16
  194.9 8.5 %collective-permute-start.2 = (bf16[2,512,128]{2,1,0:T(8,128)(2,1)S(1)}, bf16[2,512,128]{2,1,0:T(8,128)(2,1)S(1)}, u32[]{:S(2)}, u32[]{:S(2)}) collective-permute-start(bf16[2,512,128]{2,1,0:T(8,128)(2,1)S(1)} %fusion.90), channel_id=1, source_target_pairs={{28,0},{0,4},{4,8},{8,12},{12,16},{16,20},{20,24},{24,28},{29,1},{... | collective-permute-start | bytes 786440 | tf_op jit(solution)/shard_map/while/body/eval_jaxpr/ppermute | solution.py:22
  204.2 16.0 %collective-permute-start.1 = (bf16[2,512,128]{2,1,0:T(8,128)(2,1)}, bf16[2,512,128]{2,1,0:T(8,128)(2,1)S(1)}, u32[]{:S(2)}, u32[]{:S(2)}) collective-permute-start(bf16[2,512,128]{2,1,0:T(8,128)(2,1)} %copy.171), channel_id=1, source_target_pairs={{0,4},{4,8},{8,12},{12,16},{16,20},{20,24},{24,28},{1,5},{5,9},{9,... | collective-permute-start | bytes 786440 | tf_op jit(solution)/shard_map/while/body/eval_jaxpr/ppermute | solution.py:16
  212.4 7.7 %collective-permute-start.2 = (bf16[2,512,128]{2,1,0:T(8,128)(2,1)S(1)}, bf16[2,512,128]{2,1,0:T(8,128)(2,1)S(1)}, u32[]{:S(2)}, u32[]{:S(2)}) collective-permute-start(bf16[2,512,128]{2,1,0:T(8,128)(2,1)S(1)} %fusion.90), channel_id=1, source_target_pairs={{28,0},{0,4},{4,8},{8,12},{12,16},{16,20},{20,24},{24,28},{29,1},{... | collective-permute-start | bytes 786440 | tf_op jit(solution)/shard_map/while/body/eval_jaxpr/ppermute | solution.py:22
  220.9 15.2 %collective-permute-start.1 = (bf16[2,512,128]{2,1,0:T(8,128)(2,1)}, bf16[2,512,128]{2,1,0:T(8,128)(2,1)S(1)}, u32[]{:S(2)}, u32[]{:S(2)}) collective-permute-start(bf16[2,512,128]{2,1,0:T(8,128)(2,1)} %copy.171), channel_id=1, source_target_pairs={{0,4},{4,8},{8,12},{12,16},{16,20},{20,24},{24,28},{1,5},{5,9},{9,... | collective-permute-start | bytes 786440 | tf_op jit(solution)/shard_map/while/body/eval_jaxpr/ppermute | solution.py:16
  229.2 6.8 %collective-permute-start.2 = (bf16[2,512,128]{2,1,0:T(8,128)(2,1)S(1)}, bf16[2,512,128]{2,1,0:T(8,128)(2,1)S(1)}, u32[]{:S(2)}, u32[]{:S(2)}) collective-permute-start(bf16[2,512,128]{2,1,0:T(8,128)(2,1)S(1)} %fusion.90), channel_id=1, source_target_pairs={{28,0},{0,4},{4,8},{8,12},{12,16},{16,20},{20,24},{24,28},{29,1},{... | collective-permute-start | bytes 786440 | tf_op jit(solution)/shard_map/while/body/eval_jaxpr/ppermute | solution.py:22
  236.8 14.5 %collective-permute-start.1 = (bf16[2,512,128]{2,1,0:T(8,128)(2,1)}, bf16[2,512,128]{2,1,0:T(8,128)(2,1)S(1)}, u32[]{:S(2)}, u32[]{:S(2)}) collective-permute-start(bf16[2,512,128]{2,1,0:T(8,128)(2,1)} %copy.171), channel_id=1, source_target_pairs={{0,4},{4,8},{8,12},{12,16},{16,20},{20,24},{24,28},{1,5},{5,9},{9,... | collective-permute-start | bytes 786440 | tf_op jit(solution)/shard_map/while/body/eval_jaxpr/ppermute | solution.py:16
  245.2 6.1 %collective-permute-start.2 = (bf16[2,512,128]{2,1,0:T(8,128)(2,1)S(1)}, bf16[2,512,128]{2,1,0:T(8,128)(2,1)S(1)}, u32[]{:S(2)}, u32[]{:S(2)}) collective-permute-start(bf16[2,512,128]{2,1,0:T(8,128)(2,1)S(1)} %fusion.90), channel_id=1, source_target_pairs={{28,0},{0,4},{4,8},{8,12},{12,16},{16,20},{20,24},{24,28},{29,1},{... | collective-permute-start | bytes 786440 | tf_op jit(solution)/shard_map/while/body/eval_jaxpr/ppermute | solution.py:22
  252.1 14.7 %collective-permute-start.1 = (bf16[2,512,128]{2,1,0:T(8,128)(2,1)}, bf16[2,512,128]{2,1,0:T(8,128)(2,1)S(1)}, u32[]{:S(2)}, u32[]{:S(2)}) collective-permute-start(bf16[2,512,128]{2,1,0:T(8,128)(2,1)} %copy.171), channel_id=1, source_target_pairs={{0,4},{4,8},{8,12},{12,16},{16,20},{20,24},{24,28},{1,5},{5,9},{9,... | collective-permute-start | bytes 786440 | tf_op jit(solution)/shard_map/while/body/eval_jaxpr/ppermute | solution.py:16
  260.4 6.3 %collective-permute-start.2 = (bf16[2,512,128]{2,1,0:T(8,128)(2,1)S(1)}, bf16[2,512,128]{2,1,0:T(8,128)(2,1)S(1)}, u32[]{:S(2)}, u32[]{:S(2)}) collective-permute-start(bf16[2,512,128]{2,1,0:T(8,128)(2,1)S(1)} %fusion.90), channel_id=1, source_target_pairs={{28,0},{0,4},{4,8},{8,12},{12,16},{16,20},{20,24},{24,28},{29,1},{... | collective-permute-start | bytes 786440 | tf_op jit(solution)/shard_map/while/body/eval_jaxpr/ppermute | solution.py:22
  266.8 38.1 %copy-start.1 = (bf16[512,1,5,128]{0,3,2,1:T(8,128)(2,1)S(1)}, bf16[512,1,5,128]{0,3,2,1:T(8,128)(2,1)}, u32[]{:S(2)}) copy-start(bf16[512,1,5,128]{0,3,2,1:T(8,128)(2,1)} %get-tuple-element.1011) | copy-start | bytes 1966084
  292.5 7.9 %all-to-all-start.7 = ((bf16[4,128,128]{2,1,0:T(8,128)(2,1)}), bf16[4,128,128]{2,1,0:T(8,128)(2,1)S(1)}, u32[]{:S(2)}, u32[]{:S(2)}) async-start(bf16[4,128,128]{2,1,0:T(8,128)(2,1)} %bitcast.78), calls=%async_computation.7 | async-start | bytes 262144 | tf_op jit(solution)/shard_map/all_to_all | solution.py:214
  300.4 13.9 %all-to-all-start.5 = ((bf16[4,128,640]{1,2,0:T(8,128)(2,1)}), bf16[4,128,640]{1,2,0:T(8,128)(2,1)S(1)}, u32[]{:S(2)}, u32[]{:S(2)}) async-start(bf16[4,128,640]{1,2,0:T(8,128)(2,1)} %copy.124), calls=%async_computation.5 | async-start | bytes 1310720 | tf_op jit(solution)/shard_map/all_to_all | solution.py:204
  314.3 13.7 %all-to-all-start.3 = ((bf16[4,128,640]{1,2,0:T(8,128)(2,1)}), bf16[4,128,640]{1,2,0:T(8,128)(2,1)S(1)}, u32[]{:S(2)}, u32[]{:S(2)}) async-start(bf16[4,128,640]{1,2,0:T(8,128)(2,1)} %copy.118), calls=%async_computation.3 | async-start | bytes 1310720 | tf_op jit(solution)/shard_map/all_to_all | solution.py:201
where the time goes:
time: 336 us; the launch traced here: 329 us
  starting transfers between devices  106 us (32%)
  other arithmetic  67.4 us (20%)
  waiting for transfers between devices  53.6 us (16%)
  local copies, waits for them, and re-layouts  33.7 us (10%)
  matrix products  30.4 us (9%)
  blocking collectives  25 us (7%)
  loops' own time  11.2 us (3%)
    ppermute x15, starting transfers between devices, passed_along(): return lax.ppermute(value, axis, pairs)  69.9 us
    ppermute x8, waiting for transfers between devices, passed_along_2(): return lax.ppermute(block, axis, route)  27.4 us
    all_to_all x1, blocking collectives, per_device(): lax.all_to_all(grad_sums[0].astype(jnp.bfloat16), 'tp', split_axis=0, con...  25 us
    add x8, other arithmetic, backward_advance(): return (query_inner + query_part, sums_inner)  19.2 us
    reduce_or x8, other arithmetic, backward_advance(): query_part, key_value_part = lax.cond(jnp.any(visible), compute, nothing, 0)  13.8 us
    unnamed x15, local copies, waits for them, and re-layouts  13.5 us
    reduce_sum x16, other arithmetic, placed(): jnp.sum((position[:, None] >= doc_ends[None, :]).astype(jnp.int32), axis=1)  12 us
    reduce_or x7, other arithmetic, sweep_advance(): jnp.any(visible)  11.8 us
  transfers between devices with their start and end apart: 30, of which 19 were waited for; matrix products, arithmetic and copies ran while one was open for 34% of the time, Pallas kernels for 0%

commit v1 on v0

v1 whole, which is shorter than its diff:
```python
import math

import jax
import jax.numpy as jnp
from jax import lax
from jax.experimental import pallas as pl
from jax.experimental.pallas import tpu as pltpu
from jax.sharding import PartitionSpec as P

HD = 128
QH = 20
KVH = 4
GROUP = QH // KVH
HALF_Q = QH // 2
HALF_KV = KVH // 2
MESH = pl.DeviceIdType.MESH
F32 = jnp.float32
BF16 = jnp.bfloat16


def dot_nt(a, b):
    return lax.dot_general(a, b, (((1,), (1,)), ((), ())), preferred_element_type=F32)


def dot_nn(a, b):
    return lax.dot_general(a, b, (((1,), (0,)), ((), ())), preferred_element_type=F32)


def kernel(
    tp,
    window,
    planes,
    q_ref,
    k_ref,
    v_ref,
    g_ref,
    len_ref,
    o_ref,
    dq_ref,
    dk_ref,
    dv_ref,
    kv,
    qs,
    gs,
    q_stage,
    g_stage,
    kv_stage,
    psave,
    msave,
    m_cur,
    l_cur,
    acc,
    row_dot,
    dq_acc,
    bias,
    part,
    part_in,
    own_part,
    z_out,
    z_in,
    o_all,
    o_in,
    dq_all,
    dq_in,
    f_out,
    f_in,
    ex_send,
    ex_recv,
    z_sems,
    plane_send,
    plane_recv,
    part_send,
    part_recv,
    fin_send,
    fin_recv,
):
    rows = q_ref.shape[0]
    pair_rows = 2 * rows
    wide = HALF_KV * HD
    own = window
    me = lax.axis_index("seq") * tp + lax.axis_index("tp")
    core = me % 2
    pair = me // 2
    plane = pair // window
    spot = pair % window
    has_prev = plane > 0
    has_next = plane < planes - 1
    low = core == 0
    mine = pl.multiple_of(core * rows, rows)
    theirs = pl.multiple_of((1 - core) * rows, rows)

    def device(index):
        return (index // tp, index % tp)

    def chip(in_plane, which_plane):
        return device(2 * (which_plane * window + in_plane) + core)

    partner = device(2 * pair + 1 - core)

    def remote(src, dst, send_sem, recv_sem, target):
        return pltpu.make_async_remote_copy(
            src_ref=src,
            dst_ref=dst,
            send_sem=send_sem,
            recv_sem=recv_sem,
            device_id=target,
            device_id_type=MESH,
        )

    barrier = pltpu.get_barrier_semaphore()
    pl.semaphore_signal(barrier, inc=1, device_id=partner, device_id_type=MESH)
    for delta in range(1, window):
        pl.semaphore_signal(
            barrier,
            inc=1,
            device_id=chip((spot + delta) % window, plane),
            device_id_type=MESH,
        )

    @pl.when(has_prev)
    def _():
        pl.semaphore_signal(
            barrier, inc=1, device_id=chip(spot, plane - 1), device_id_type=MESH
        )

    @pl.when(has_next)
    def _():
        pl.semaphore_signal(
            barrier, inc=1, device_id=chip(spot, plane + 1), device_id_type=MESH
        )

    k_all = k_ref[...]
    v_all = v_ref[...]
    kv_stage[0] = jnp.where(low, k_all[:, wide:], k_all[:, :wide])
    kv_stage[1] = jnp.where(low, v_all[:, wide:], v_all[:, :wide])
    kv[own, 0, pl.ds(mine, rows), :] = jnp.where(low, k_all[:, :wide], k_all[:, wide:])
    kv[own, 1, pl.ds(mine, rows), :] = jnp.where(low, v_all[:, :wide], v_all[:, wide:])
    for stage, held, ref in ((q_stage, qs, q_ref), (g_stage, gs, g_ref)):
        for head in range(HALF_Q):
            left = ref[:, head * HD : (head + 1) * HD]
            right = ref[:, (head + HALF_Q) * HD : (head + HALF_Q + 1) * HD]
            stage[head] = jnp.where(low, right, left)
            held[head, pl.ds(mine, rows), :] = jnp.where(low, left, right)

    neighbours = has_prev.astype(jnp.int32) + has_next.astype(jnp.int32)
    pl.semaphore_wait(barrier, window + neighbours)

    kv_swap = remote(
        kv_stage,
        kv.at[own, :, pl.ds(mine, rows), :],
        ex_send.at[0],
        ex_recv.at[0],
        partner,
    )
    q_swap = remote(
        q_stage, qs.at[:, pl.ds(mine, rows), :], ex_send.at[1], ex_recv.at[1], partner
    )
    g_swap = remote(
        g_stage, gs.at[:, pl.ds(mine, rows), :], ex_send.at[2], ex_recv.at[2], partner
    )
    kv_swap.start()
    q_swap.start()
    kv_swap.wait_recv()

    z_send_copy = remote(
        kv.at[own], kv.at[spot], z_sems.at[0], z_sems.at[1], chip(spot, plane + 1)
    )
    z_recv_copy = remote(
        kv.at[own], kv.at[spot], z_sems.at[0], z_sems.at[1], partner
    )

    @pl.when(has_next)
    def _():
        z_send_copy.start()

    def plane_copy(delta, source):
        return remote(
            source,
            kv.at[spot],
            plane_send.at[delta],
            plane_recv.at[spot],
            chip((spot + delta) % window, plane),
        )

    for delta in range(1, window):

        @pl.when(spot + delta < window)
        def _(delta=delta):
            plane_copy(delta, kv.at[own]).start()

    g_swap.start()

    ends = []
    total = jnp.int32(0)
    for doc in range(len_ref.shape[0]):
        total = total + len_ref[doc]
        ends.append(total)
    query_pos = pair * pair_rows + lax.broadcasted_iota(jnp.int32, (1, pair_rows), 1)
    first_key = jnp.zeros((1, pair_rows), jnp.int32)
    for end in ends:
        first_key = jnp.where(query_pos >= end, end, first_key)

    factor2 = HD ** (-0.5) * math.log2(math.e)
    scaling = HD ** (-0.5)

    def absorb(slot, block, first):
        key_pos = block * pair_rows + lax.broadcasted_iota(
            jnp.int32, (pair_rows, pair_rows), 0
        )
        bias[...] = jnp.where(
            (key_pos <= query_pos) & (key_pos >= first_key), 0.0, -1e30
        )
        for kv_head in range(HALF_KV):
            columns = slice(kv_head * HD, (kv_head + 1) * HD)
            key_block = kv[slot, 0, :, columns]
            value_turned = kv[slot, 1, :, columns].T
            for within in range(GROUP):
                head = kv_head * GROUP + within
                score = dot_nt(key_block, qs[head]) * factor2 + bias[...]
                newest = jnp.max(score, axis=0, keepdims=True)
                if not first:
                    newest = jnp.maximum(m_cur[head], newest)
                weight = jnp.exp2(score - newest)
                row_sum = jnp.sum(weight, axis=0, keepdims=True)
                weight_bf = weight.astype(BF16)
                psave[slot, head] = weight_bf
                msave[slot, head] = newest
                product = dot_nn(value_turned, weight_bf)
                if first:
                    l_cur[head] = row_sum
                    acc[head] = product
                else:
                    shrink = jnp.exp2(m_cur[head] - newest)
                    l_cur[head] = l_cur[head] * shrink + row_sum
                    acc[head] = acc[head] * shrink + product
                m_cur[head] = newest

    q_swap.wait_recv()
    absorb(own, pair, True)

    @pl.when(has_prev)
    def _():
        z_recv_copy.wait_recv()
        for delta in range(1, window):

            @pl.when(spot + delta >= window)
            def _(delta=delta):
                plane_copy(delta, kv.at[spot]).start()

    def forward_step(turn, carried):
        slot = jnp.where(turn < spot, spot - 1 - turn, turn)

        @pl.when((slot < spot) | has_prev)
        def _():
            @pl.when(slot != spot)
            def _():
                remote(
                    kv.at[own],
                    kv.at[slot],
                    plane_send.at[0],
                    plane_recv.at[slot],
                    partner,
                ).wait_recv()

            block = jnp.where(slot < spot, plane, plane - 1) * window + slot
            absorb(slot, block, False)

        return carried

    lax.fori_loop(0, window, forward_step, 0)
    g_swap.wait_recv()

    for head in range(HALF_Q):
        inverse = 1.0 / l_cur[head]
        out_turned = acc[head] * inverse
        o_all[head] = out_turned.T.astype(BF16)
        grad_turned = gs[head].astype(F32).T
        row_dot[head] = jnp.sum(
            grad_turned * out_turned.astype(BF16).astype(F32), axis=0, keepdims=True
        )
        l_cur[head] = inverse
        dq_acc[head] = jnp.zeros((HD, pair_rows), F32)

    o_swap = remote(
        o_all.at[:, pl.ds(theirs, rows), :], o_in, fin_send.at[0], fin_recv.at[0], partner
    )
    o_swap.start()

    def contribute(slot, put):
        for kv_head in range(HALF_KV):
            columns = slice(kv_head * HD, (kv_head + 1) * HD)
            key_turned = kv[slot, 0, :, columns].T
            value_block = kv[slot, 1, :, columns]
            key_sum = jnp.zeros((pair_rows, HD), F32)
            value_sum = jnp.zeros((pair_rows, HD), F32)
            for within in range(GROUP):
                head = kv_head * GROUP + within
                level = jnp.exp2(msave[slot, head] - m_cur[head]) * l_cur[head]
                probability = psave[slot, head].astype(F32) * level
                grad_prob = dot_nt(value_block, gs[head])
                grad_score = (probability * (grad_prob - row_dot[head])).astype(BF16)
                value_sum = value_sum + dot_nn(probability.astype(BF16), gs[head])
                key_sum = key_sum + dot_nn(grad_score, qs[head])
                dq_acc[head] = dq_acc[head] + dot_nn(key_turned, grad_score)
            put(0, columns, key_sum * scaling)
            put(1, columns, value_sum)

    def part_copy(slot):
        return remote(
            part.at[slot],
            part_in.at[spot],
            part_send.at[slot],
            part_recv.at[spot],
            chip(slot, plane),
        )

    def backward_step(turn, carried):
        slot = window - 1 - turn

        @pl.when((slot < spot) | has_prev)
        def _():
            def put(which, columns, value):
                part[slot, which, :, columns] = value.astype(BF16)

            contribute(slot, put)

            @pl.when(slot != spot)
            def _():
                part_copy(slot).start()

        return carried

    lax.fori_loop(0, window, backward_step, 0)

    def part_arrived(slot):
        remote(
            part.at[slot], part_in.at[slot], part_send.at[slot], part_recv.at[slot], partner
        ).wait_recv()

    z_back = remote(z_out, z_in, z_sems.at[2], z_sems.at[3], chip(spot, plane - 1))
    z_back_in = remote(z_out, z_in, z_sems.at[2], z_sems.at[3], partner)

    @pl.when(has_prev)
    def _():
        own_part[...] = part[spot].astype(F32)

        def gather(slot, carried):
            part_arrived(slot)
            own_part[...] += part_in[slot].astype(F32)
            return carried

        lax.fori_loop(0, spot, gather, 0)
        z_out[...] = own_part[...].astype(BF16)
        z_back.start()

    def put_own(which, columns, value):
        own_part[which, :, columns] = value

    contribute(own, put_own)

    for head in range(HALF_Q):
        dq_all[head] = (dq_acc[head] * scaling).T.astype(BF16)
    dq_swap = remote(
        dq_all.at[:, pl.ds(theirs, rows), :],
        dq_in,
        fin_send.at[1],
        fin_recv.at[1],
        partner,
    )
    dq_swap.start()

    def gather_own(slot, carried):
        part_arrived(slot)
        own_part[...] += part_in[slot].astype(F32)
        return carried

    lax.fori_loop(spot + 1, window, gather_own, 0)

    o_swap.wait_recv()
    dq_swap.wait_recv()
    for ref, everything, arrived in ((o_ref, o_all, o_in), (dq_ref, dq_all, dq_in)):
        for head in range(HALF_Q):
            here = everything[head, pl.ds(mine, rows), :]
            there = arrived[head]
            ref[:, head * HD : (head + 1) * HD] = jnp.where(low, here, there)
            ref[:, (head + HALF_Q) * HD : (head + HALF_Q + 1) * HD] = jnp.where(
                low, there, here
            )

    @pl.when(has_next)
    def _():
        z_back_in.wait_recv()
        own_part[...] += z_in[...].astype(F32)

    f_out[...] = own_part[:, pl.ds(theirs, rows), :].astype(BF16)
    f_swap = remote(f_out, f_in, fin_send.at[2], fin_recv.at[2], partner)
    f_swap.start()
    f_swap.wait_recv()
    for which, ref in ((0, dk_ref), (1, dv_ref)):
        here = own_part[which, pl.ds(mine, rows), :].astype(BF16)
        there = f_in[which]
        ref[:, :wide] = jnp.where(low, here, there)
        ref[:, wide:] = jnp.where(low, there, here)

    for copy in (kv_swap, q_swap, g_swap, o_swap, dq_swap, f_swap):
        copy.wait_send()

    @pl.when(has_next)
    def _():
        z_send_copy.wait_send()

    @pl.when(has_prev)
    def _():
        z_back.wait_send()

    for delta in range(1, window):

        @pl.when((spot + delta < window) | has_prev)
        def _(delta=delta):
            plane_copy(delta, kv.at[own]).wait_send()

    def sent(slot, carried):
        @pl.when(((slot < spot) | has_prev) & (slot != spot))
        def _():
            part_copy(slot).wait_send()

        return carried

    lax.fori_loop(0, window, sent, 0)


def per_device(seq, tp, query_rows, key_rows, value_rows, out_grad, doc_lengths):
    rows = query_rows.shape[0]
    pairs = seq * tp // 2
    planes = 4
    window = pairs // planes
    pair_rows = 2 * rows
    wide = HALF_KV * HD
    blocks = window + 1
    dma = pltpu.SemaphoreType.DMA
    vmem = pltpu.VMEM
    scratch = [
        vmem((blocks, 2, pair_rows, wide), BF16),
        vmem((HALF_Q, pair_rows, HD), BF16),
        vmem((HALF_Q, pair_rows, HD), BF16),
        vmem((HALF_Q, rows, HD), BF16),
        vmem((HALF_Q, rows, HD), BF16),
        vmem((2, rows, wide), BF16),
        vmem((blocks, HALF_Q, pair_rows, pair_rows), BF16),
        vmem((blocks, HALF_Q, 1, pair_rows), F32),
        vmem((HALF_Q, 1, pair_rows), F32),
        vmem((HALF_Q, 1, pair_rows), F32),
        vmem((HALF_Q, HD, pair_rows), F32),
        vmem((HALF_Q, 1, pair_rows), F32),
        vmem((HALF_Q, HD, pair_rows), F32),
        vmem((pair_rows, pair_rows), F32),
        vmem((window, 2, pair_rows, wide), BF16),
        vmem((window, 2, pair_rows, wide), BF16),
        vmem((2, pair_rows, wide), F32),
        vmem((2, pair_rows, wide), BF16),
        vmem((2, pair_rows, wide), BF16),
        vmem((HALF_Q, pair_rows, HD), BF16),
        vmem((HALF_Q, rows, HD), BF16),
        vmem((HALF_Q, pair_rows, HD), BF16),
        vmem((HALF_Q, rows, HD), BF16),
        vmem((2, rows, wide), BF16),
        vmem((2, rows, wide), BF16),
        dma((3,)),
        dma((3,)),
        dma((4,)),
        dma((window,)),
        dma((window,)),
        dma((window,)),
        dma((window,)),
        dma((3,)),
        dma((3,)),
    ]
    whole = pl.BlockSpec(memory_space=pltpu.VMEM)

    def body(*refs):
        kernel(tp, window, planes, *refs)

    return pl.pallas_call(
        body,
        out_shape=tuple(
            jax.ShapeDtypeStruct(x.shape, BF16)
            for x in (query_rows, query_rows, key_rows, value_rows)
        ),
        in_specs=[whole] * 4 + [pl.BlockSpec(memory_space=pltpu.SMEM)],
        out_specs=(whole,) * 4,
        scratch_shapes=scratch,
        compiler_params=pltpu.CompilerParams(
            collective_id=0,
            has_side_effects=True,
            vmem_limit_bytes=60 * 2**20,
        ),
        name="packed_attention",
    )(query_rows, key_rows, value_rows, out_grad, doc_lengths)


def solution(mesh):
    seq, tp = mesh.shape["seq"], mesh.shape["tp"]
    spec = P(("seq", "tp"), None)

    def run(*args):
        return per_device(seq, tp, *args)

    return jax.shard_map(
        run,
        mesh=mesh,
        in_specs=(spec, spec, spec, spec, P()),
        out_specs=(spec,) * 4,
        check_vma=False,
    )
```

time: 336 us -> 63.1 us (0.19); the launches traced: 329 us -> 62.9 us
  starting transfers between devices: 106 us -> 0 us
  other arithmetic: 67.4 us -> 0 us
  Pallas kernels: 0 us -> 57.5 us
  waiting for transfers between devices: 53.6 us -> 0 us
  matrix products: 30.4 us -> 0 us
  local copies, waits for them, and re-layouts: 33.7 us -> 4.66 us
  blocking collectives: 25 us -> 0 us
  loops' own time: 11.2 us -> 0 us
    ppermute x23 -> x0, starting transfers between devices: 75.7 us -> none  [the longest x15 69.9 us: passed_along(): return lax.ppermute(value, axis, pairs)]
    pallas_call x0 -> x1, Pallas kernels: none -> 57.5 us  [per_device(): pl.pallas_call(body, out_shape=tuple((jax.ShapeDtypeStruct(x.shape, BF16)...]
    ppermute x23 -> x0, waiting for transfers between devices: 34.4 us -> none  [the longest x8 27.4 us: passed_along_2(): return lax.ppermute(block, axis, route)]
    all_to_all x7 -> x0, starting transfers between devices: 30.7 us -> none  [the longest x1 4.96 us: per_device(): lax.all_to_all(out_grad, 'tp', split_axis=1, concat_axis=0, tiled=True)]
    dot_general x14 -> x0, matrix products: 30.4 us -> none  [the longest x2 9.56 us: absorb(): jnp.einsum('bkgt,tkd->bkgd', weight.astype(jnp.bfloat16), value_block, pr...]
    reduce_or x15 -> x0, other arithmetic: 25.6 us -> none  [the longest x8 13.8 us: backward_advance(): query_part, key_value_part = lax.cond(jnp.any(visible), compute, nothing, 0)]
    all_to_all x1 -> x0, blocking collectives: 25 us -> none  [per_device(): lax.all_to_all(grad_sums[0].astype(jnp.bfloat16), 'tp', split_axis=0, con...]
    add x42 -> x0, other arithmetic: 19.9 us -> none  [the longest x8 19.2 us: backward_advance(): return (query_inner + query_part, sums_inner)]
  transfers between devices with their start and end apart: 30 -> 0, of which waited for: 19 -> 0; matrix products, arithmetic and copies ran while one was open for 34% -> 0% of each run, Pallas kernels for 0% -> 0%
where the time goes in v1:
time: 63.1 us; the launch traced here: 62.9 us
  Pallas kernels  57.5 us (91%)
  local copies, waits for them, and re-layouts  4.66 us (7%)
  between operations  0.65 us (1%)
    pallas_call x1, Pallas kernels, per_device(): pl.pallas_call(body, out_shape=tuple((jax.ShapeDtypeStruct(x.shape, BF16)...  57.5 us
    unnamed x10, local copies, waits for them, and re-layouts  4.66 us

profile of v1, /device:TPU:13, one launch (start us, length us, event | category | flops | bytes accessed | tf_op | source)
XLA Modules:
  0.0 62.9 jit_solution(9508384868549804675)
XLA Ops:
  0.6 57.5 %packed_attention.1 = (bf16[128,2560]{1,0:T(8,128)(2,1)}, bf16[128,2560]{1,0:T(8,128)(2,1)}, bf16[128,512]{1,0:T(8,128)(2,1)}, bf16[128,512]{1,0:T(8,128)(2,1)}) custom-call(bf16[128,2560]{1,0:T(8,128)(2,1)} %refs_0_.1, bf16[128,512]{1,0:T(8,128)(2,1)} %refs_1_.1, bf16[128,512]{1,0:T(8,128)(2,1)} %refs_2_.1, bf16[128,2560]{1,0:T(8,128)(2,1)} %refs_3_.1, ...), custom_call_target="tpu_custom_call" | custom-call | tf_op jit(solution)/shard_map/packed_attention/pallas_call | solution.py:483
  58.2 0.0 copy-start
  58.2 2.0 %copy.13 = bf16[128,2560]{1,0:T(8,128)(2,1)} copy(bf16[128,2560]{1,0:T(8,128)(2,1)} %get-tuple-element.8) | data formatting | bytes 1310720
  60.2 0.0 copy-done
  60.2 0.0 copy-start.2
  60.2 0.8 %copy.14 = bf16[128,2560]{1,0:T(8,128)(2,1)} copy(bf16[128,2560]{1,0:T(8,128)(2,1)S(1)} %copy-done) | data formatting | bytes 1310720
  61.1 0.2 copy-done.2
  61.2 0.0 copy-start.1
  61.2 0.7 %copy.15 = bf16[128,512]{1,0:T(8,128)(2,1)} copy(bf16[128,512]{1,0:T(8,128)(2,1)S(1)} %copy-done.2) | data formatting | bytes 262144
  61.9 0.3 copy-done.1
  62.2 0.7 %copy.16 = bf16[128,512]{1,0:T(8,128)(2,1)} copy(bf16[128,512]{1,0:T(8,128)(2,1)S(1)} %copy-done.1) | data formatting | bytes 262144
Async XLA Ops:
  58.2 2.0 %copy-start = (bf16[128,2560]{1,0:T(8,128)(2,1)S(1)}, bf16[128,2560]{1,0:T(8,128)(2,1)}, u32[]{:S(2)}) copy-start(bf16[128,2560]{1,0:T(8,128)(2,1)} %get-tuple-element.9) | copy-start | bytes 1966084
  60.2 1.0 %copy-start.2 = (bf16[128,512]{1,0:T(8,128)(2,1)S(1)}, bf16[128,512]{1,0:T(8,128)(2,1)}, u32[]{:S(2)}) copy-start(bf16[128,512]{1,0:T(8,128)(2,1)} %get-tuple-element.10) | copy-start | bytes 393220
  61.2 1.0 %copy-start.1 = (bf16[128,512]{1,0:T(8,128)(2,1)S(1)}, bf16[128,512]{1,0:T(8,128)(2,1)}, u32[]{:S(2)}) copy-start(bf16[128,512]{1,0:T(8,128)(2,1)} %get-tuple-element.11) | copy-start | bytes 393220

commit v2 on v1

--- a/solution.py
+++ b/solution.py
@@ -13,6 +13,7 @@
 GROUP = QH // KVH
 HALF_Q = QH // 2
 HALF_KV = KVH // 2
+CHUNK = 128
 MESH = pl.DeviceIdType.MESH
 F32 = jnp.float32
 BF16 = jnp.bfloat16
@@ -49,10 +50,16 @@
     msave,
     m_cur,
     l_cur,
+    shrinks,
     acc,
     row_dot,
     dq_acc,
     bias,
+    q_turned,
+    g_turned,
+    wide_buf,
+    p_buf,
+    ds_buf,
     part,
     part_in,
     own_part,
@@ -97,6 +104,10 @@
 
     partner = device(2 * pair + 1 - core)
 
+    def head_lanes(head):
+        kv_head, within = divmod(head, GROUP)
+        return kv_head, slice(within * pair_rows, (within + 1) * pair_rows)
+
     def remote(src, dst, send_sem, recv_sem, target):
         return pltpu.make_async_remote_copy(
             src_ref=src,
@@ -212,30 +223,37 @@
         )
         for kv_head in range(HALF_KV):
             columns = slice(kv_head * HD, (kv_head + 1) * HD)
-            key_block = kv[slot, 0, :, columns]
-            value_turned = kv[slot, 1, :, columns].T
-            for within in range(GROUP):
-                head = kv_head * GROUP + within
-                score = dot_nt(key_block, qs[head]) * factor2 + bias[...]
+            wide_buf[kv_head] = dot_nn(kv[slot, 0, :, columns], q_turned[kv_head])
+        for kv_head in range(HALF_KV):
+            columns = slice(kv_head * HD, (kv_head + 1) * HD)
+            for at in range(0, GROUP * pair_rows, CHUNK):
+                lanes = slice(at, at + CHUNK)
+                tokens = slice(at % pair_rows, at % pair_rows + CHUNK)
+                score = wide_buf[kv_head, :, lanes] * factor2 + bias[:, tokens]
                 newest = jnp.max(score, axis=0, keepdims=True)
                 if not first:
-                    newest = jnp.maximum(m_cur[head], newest)
+                    before = m_cur[kv_head, :, lanes]
+                    newest = jnp.maximum(before, newest)
                 weight = jnp.exp2(score - newest)
                 row_sum = jnp.sum(weight, axis=0, keepdims=True)
-                weight_bf = weight.astype(BF16)
-                psave[slot, head] = weight_bf
-                msave[slot, head] = newest
-                product = dot_nn(value_turned, weight_bf)
-                if first:
-                    l_cur[head] = row_sum
-                    acc[head] = product
-                else:
-                    shrink = jnp.exp2(m_cur[head] - newest)
-                    l_cur[head] = l_cur[head] * shrink + row_sum
-                    acc[head] = acc[head] * shrink + product
-                m_cur[head] = newest
+                psave[slot, kv_head, :, lanes] = weight.astype(BF16)
+                msave[slot, kv_head, :, lanes] = newest
+                if not first:
+                    shrink = jnp.exp2(before - newest)
+                    row_sum = l_cur[kv_head, :, lanes] * shrink + row_sum
+                    shrinks[kv_head, :, lanes] = shrink
+                l_cur[kv_head, :, lanes] = row_sum
+                m_cur[kv_head, :, lanes] = newest
+            product = dot_nn(kv[slot, 1, :, columns].T, psave[slot, kv_head])
+            if first:
+                acc[kv_head] = product
+            else:
+                acc[kv_head] = acc[kv_head] * shrinks[kv_head] + product
 
     q_swap.wait_recv()
+    for head in range(HALF_Q):
+        kv_head, lanes = head_lanes(head)
+        q_turned[kv_head, :, lanes] = qs[head].T
     absorb(own, pair, True)
 
     @pl.when(has_prev)
@@ -271,15 +289,19 @@
     g_swap.wait_recv()
 
     for head in range(HALF_Q):
-        inverse = 1.0 / l_cur[head]
-        out_turned = acc[head] * inverse
+        kv_head, lanes = head_lanes(head)
+        inverse = 1.0 / l_cur[kv_head, :, lanes]
+        out_turned = acc[kv_head, :, lanes] * inverse
         o_all[head] = out_turned.T.astype(BF16)
-        grad_turned = gs[head].astype(F32).T
-        row_dot[head] = jnp.sum(
-            grad_turned * out_turned.astype(BF16).astype(F32), axis=0, keepdims=True
-        )
-        l_cur[head] = inverse
-        dq_acc[head] = jnp.zeros((HD, pair_rows), F32)
+        grad_turned = gs[head].T
+        g_turned[kv_head, :, lanes] = grad_turned
+        row_dot[kv_head, :, lanes] = jnp.sum(
+            grad_turned.astype(F32) * out_turned.astype(BF16).astype(F32),
+            axis=0,
+            keepdims=True,
+        )
+        l_cur[kv_head, :, lanes] = inverse
+    dq_acc[...] = jnp.zeros_like(dq_acc)
 
     o_swap = remote(
         o_all.at[:, pl.ds(theirs, rows), :], o_in, fin_send.at[0], fin_recv.at[0], partner
@@ -289,21 +311,31 @@
     def contribute(slot, put):
         for kv_head in range(HALF_KV):
             columns = slice(kv_head * HD, (kv_head + 1) * HD)
-            key_turned = kv[slot, 0, :, columns].T
-            value_block = kv[slot, 1, :, columns]
-            key_sum = jnp.zeros((pair_rows, HD), F32)
-            value_sum = jnp.zeros((pair_rows, HD), F32)
-            for within in range(GROUP):
-                head = kv_head * GROUP + within
-                level = jnp.exp2(msave[slot, head] - m_cur[head]) * l_cur[head]
-                probability = psave[slot, head].astype(F32) * level
-                grad_prob = dot_nt(value_block, gs[head])
-                grad_score = (probability * (grad_prob - row_dot[head])).astype(BF16)
-                value_sum = value_sum + dot_nn(probability.astype(BF16), gs[head])
-                key_sum = key_sum + dot_nn(grad_score, qs[head])
-                dq_acc[head] = dq_acc[head] + dot_nn(key_turned, grad_score)
-            put(0, columns, key_sum * scaling)
-            put(1, columns, value_sum)
+            wide_buf[kv_head] = dot_nn(kv[slot, 1, :, columns], g_turned[kv_head])
+        for kv_head in range(HALF_KV):
+            columns = slice(kv_head * HD, (kv_head + 1) * HD)
+            heads = slice(kv_head * GROUP, (kv_head + 1) * GROUP)
+            stacked = (GROUP * pair_rows, HD)
+            for at in range(0, GROUP * pair_rows, CHUNK):
+                lanes = slice(at, at + CHUNK)
+                level = (
+                    jnp.exp2(msave[slot, kv_head, :, lanes] - m_cur[kv_head, :, lanes])
+                    * l_cur[kv_head, :, lanes]
+                )
+                probability = psave[slot, kv_head, :, lanes].astype(F32) * level
+                grad_prob = wide_buf[kv_head, :, lanes]
+                grad_score = probability * (grad_prob - row_dot[kv_head, :, lanes])
+                p_buf[kv_head, :, lanes] = probability.astype(BF16)
+                ds_buf[kv_head, :, lanes] = grad_score.astype(BF16)
+            put(1, columns, dot_nn(p_buf[kv_head], gs[heads].reshape(stacked)))
+            put(
+                0,
+                columns,
+                dot_nn(ds_buf[kv_head], qs[heads].reshape(stacked)) * scaling,
+            )
+            dq_acc[kv_head] = dq_acc[kv_head] + dot_nn(
+                kv[slot, 0, :, columns].T, ds_buf[kv_head]
+            )
 
     def part_copy(slot):
         return remote(
@@ -359,7 +391,8 @@
     contribute(own, put_own)
 
     for head in range(HALF_Q):
-        dq_all[head] = (dq_acc[head] * scaling).T.astype(BF16)
+        kv_head, lanes = head_lanes(head)
+        dq_all[head] = (dq_acc[kv_head, :, lanes] * scaling).T.astype(BF16)
     dq_swap = remote(
         dq_all.at[:, pl.ds(theirs, rows), :],
         dq_in,
@@ -429,6 +462,11 @@
     lax.fori_loop(0, window, sent, 0)
 
 
+def hand_over(*refs):
+    for source, target in zip(refs[:4], refs[4:]):
+        target[...] = source[...]
+
+
 def per_device(seq, tp, query_rows, key_rows, value_rows, out_grad, doc_lengths):
     rows = query_rows.shape[0]
     pairs = seq * tp // 2
@@ -437,6 +475,7 @@
     pair_rows = 2 * rows
     wide = HALF_KV * HD
     blocks = window + 1
+    long = GROUP * pair_rows
     dma = pltpu.SemaphoreType.DMA
     vmem = pltpu.VMEM
     scratch = [
@@ -446,14 +485,20 @@
         vmem((HALF_Q, rows, HD), BF16),
         vmem((HALF_Q, rows, HD), BF16),
         vmem((2, rows, wide), BF16),
-        vmem((blocks, HALF_Q, pair_rows, pair_rows), BF16),
-        vmem((blocks, HALF_Q, 1, pair_rows), F32),
-        vmem((HALF_Q, 1, pair_rows), F32),
-        vmem((HALF_Q, 1, pair_rows), F32),
-        vmem((HALF_Q, HD, pair_rows), F32),
-        vmem((HALF_Q, 1, pair_rows), F32),
-        vmem((HALF_Q, HD, pair_rows), F32),
+        vmem((blocks, HALF_KV, pair_rows, long), BF16),
+        vmem((blocks, HALF_KV, 1, long), F32),
+        vmem((HALF_KV, 1, long), F32),
+        vmem((HALF_KV, 1, long), F32),
+        vmem((HALF_KV, 1, long), F32),
+        vmem((HALF_KV, HD, long), F32),
+        vmem((HALF_KV, 1, long), F32),
+        vmem((HALF_KV, HD, long), F32),
         vmem((pair_rows, pair_rows), F32),
+        vmem((HALF_KV, HD, long), BF16),
+        vmem((HALF_KV, HD, long), BF16),
+        vmem((HALF_KV, pair_rows, long), F32),
+        vmem((HALF_KV, pair_rows, long), BF16),
+        vmem((HALF_KV, pair_rows, long), BF16),
         vmem((window, 2, pair_rows, wide), BF16),
         vmem((window, 2, pair_rows, wide), BF16),
         vmem((2, pair_rows, wide), F32),
@@ -480,12 +525,13 @@
     def body(*refs):
         kernel(tp, window, planes, *refs)
 
-    return pl.pallas_call(
+    shapes = tuple(
+        jax.ShapeDtypeStruct(x.shape, BF16)
+        for x in (query_rows, query_rows, key_rows, value_rows)
+    )
+    results = pl.pallas_call(
         body,
-        out_shape=tuple(
-            jax.ShapeDtypeStruct(x.shape, BF16)
-            for x in (query_rows, query_rows, key_rows, value_rows)
-        ),
+        out_shape=shapes,
         in_specs=[whole] * 4 + [pl.BlockSpec(memory_space=pltpu.SMEM)],
         out_specs=(whole,) * 4,
         scratch_shapes=scratch,
@@ -496,6 +542,13 @@
         ),
         name="packed_attention",
     )(query_rows, key_rows, value_rows, out_grad, doc_lengths)
+    return pl.pallas_call(
+        hand_over,
+        out_shape=shapes,
+        in_specs=[whole] * 4,
+        out_specs=(whole,) * 4,
+        name="hand_over",
+    )(*results)
 
 
 def solution(mesh):

time: 63.1 us -> 58 us (0.919)
  local copies, waits for them, and re-layouts: 4.66 us -> 0 us
    unnamed x10 -> x0, local copies, waits for them, and re-layouts: 4.66 us -> none
    pallas_call x1 -> x2, Pallas kernels: 57.5 us -> 57.2 us  [the longest x1 54.7 us: per_device(): pl.pallas_call(body, out_shape=shapes, in_specs=[whole] * 4 + [pl.BlockSp...]
where the time goes in v2:
time: 58 us; the launch traced here: 57.9 us
  Pallas kernels  57.2 us (99%)
  between operations  0.64 us (1%)
    pallas_call x1, Pallas kernels, per_device(): pl.pallas_call(body, out_shape=shapes, in_specs=[whole] * 4 + [pl.BlockSp...  54.7 us
    pallas_call x1, Pallas kernels, per_device(): pl.pallas_call(hand_over, out_shape=shapes, in_specs=[whole] * 4, out_spe...  2.51 us

profile of v2, /device:TPU:13, one launch (start us, length us, event | category | flops | bytes accessed | tf_op | source)
XLA Modules:
  0.0 57.9 jit_solution(989421542648646845)
XLA Ops:
  0.6 54.7 %packed_attention.1 = (bf16[128,2560]{1,0:T(8,128)(2,1)}, bf16[128,2560]{1,0:T(8,128)(2,1)}, bf16[128,512]{1,0:T(8,128)(2,1)}, bf16[128,512]{1,0:T(8,128)(2,1)}) custom-call(bf16[128,2560]{1,0:T(8,128)(2,1)} %refs_0_.1, bf16[128,512]{1,0:T(8,128)(2,1)} %refs_1_.1, bf16[128,512]{1,0:T(8,128)(2,1)} %refs_2_.1, bf16[128,2560]{1,0:T(8,128)(2,1)} %refs_3_.1, ...), custom_call_target="tpu_custom_call" | custom-call | tf_op jit(solution)/shard_map/packed_attention/pallas_call | solution.py:532
  55.3 2.5 %hand_over.1 = (bf16[128,2560]{1,0:T(8,128)(2,1)}, bf16[128,2560]{1,0:T(8,128)(2,1)}, bf16[128,512]{1,0:T(8,128)(2,1)}, bf16[128,512]{1,0:T(8,128)(2,1)}) custom-call(bf16[128,2560]{1,0:T(8,128)(2,1)} %get-tuple-element.8.refs_0_, bf16[128,2560]{1,0:T(8,128)(2,1)} %get-tuple-element.9.refs_1_, bf16[128,512]{1,0:T(8,128)(2,1)} %get-tuple-element.10.refs_2_, ...), custom_call_target="tpu_custom_call" | custom-call | tf_op jit(solution)/shard_map/hand_over/pallas_call | solution.py:545

commit v3 on v2

--- a/solution.py
+++ b/solution.py
@@ -63,6 +63,7 @@
     part,
     part_in,
     own_part,
+    totals,
     z_out,
     z_in,
     o_all,
@@ -73,7 +74,9 @@
     f_in,
     ex_send,
     ex_recv,
-    z_sems,
+    z_send,
+    z_recv,
+    z_back_sems,
     plane_send,
     plane_recv,
     part_send,
@@ -99,8 +102,8 @@
     def device(index):
         return (index // tp, index % tp)
 
-    def chip(in_plane, which_plane):
-        return device(2 * (which_plane * window + in_plane) + core)
+    def at_chip(in_plane, which_plane, which_core):
+        return device(2 * (which_plane * window + in_plane) + which_core)
 
     partner = device(2 * pair + 1 - core)
 
@@ -119,87 +122,112 @@
         )
 
     barrier = pltpu.get_barrier_semaphore()
-    pl.semaphore_signal(barrier, inc=1, device_id=partner, device_id_type=MESH)
-    for delta in range(1, window):
-        pl.semaphore_signal(
-            barrier,
-            inc=1,
-            device_id=chip((spot + delta) % window, plane),
-            device_id_type=MESH,
-        )
-
-    @pl.when(has_prev)
-    def _():
-        pl.semaphore_signal(
-            barrier, inc=1, device_id=chip(spot, plane - 1), device_id_type=MESH
-        )
+
+    def greet(target):
+        pl.semaphore_signal(barrier, inc=1, device_id=target, device_id_type=MESH)
+
+    greet(partner)
+    for which in range(2):
+        for delta in range(1, window):
+            greet(at_chip((spot + delta) % window, plane, which))
+
+        @pl.when(has_prev)
+        def _(which=which):
+            greet(at_chip(spot, plane - 1, which))
+
+        @pl.when(has_next)
+        def _(which=which):
+            greet(at_chip(spot, plane + 1, which))
+
+    k_all = k_ref[...]
+    v_all = v_ref[...]
+    for which in range(2):
+        half = slice(which * wide, (which + 1) * wide)
+        kv_stage[which, 0] = k_all[:, half]
+        kv_stage[which, 1] = v_all[:, half]
+    kv[own, 0, pl.ds(mine, rows), :] = jnp.where(low, k_all[:, :wide], k_all[:, wide:])
+    kv[own, 1, pl.ds(mine, rows), :] = jnp.where(low, v_all[:, :wide], v_all[:, wide:])
+
+    neighbours = has_prev.astype(jnp.int32) + has_next.astype(jnp.int32)
+    pl.semaphore_wait(barrier, 2 * window - 1 + 2 * neighbours)
+
+    def z_copy(which, part_of):
+        return remote(
+            kv_stage.at[which, part_of],
+            kv.at[spot, part_of, pl.ds(mine, rows), :],
+            z_send.at[which, part_of],
+            z_recv.at[core, part_of],
+            at_chip(spot, plane + 1, which),
+        )
+
+    def z_arrival(row_core, part_of):
+        return remote(
+            kv_stage.at[0, part_of],
+            kv.at[spot, part_of, pl.ds(row_core * rows, rows), :],
+            z_send.at[0, part_of],
+            z_recv.at[row_core, part_of],
+            partner,
+        )
+
+    def plane_copy(delta, which):
+        return remote(
+            kv_stage.at[which],
+            kv.at[spot, :, pl.ds(mine, rows), :],
+            plane_send.at[delta, which],
+            plane_recv.at[spot, core],
+            at_chip((spot + delta) % window, plane, which),
+        )
+
+    def plane_pass(delta, part_of):
+        return remote(
+            kv.at[spot, part_of],
+            kv.at[spot, part_of],
+            plane_send.at[delta, part_of],
+            plane_recv.at[spot, part_of],
+            at_chip((spot + delta) % window, plane, core),
+        )
+
+    kv_swap = remote(
+        kv_stage.at[1 - core],
+        kv.at[own, :, pl.ds(mine, rows), :],
+        ex_send.at[0],
+        ex_recv.at[0],
+        partner,
+    )
+    kv_swap.start()
 
     @pl.when(has_next)
     def _():
-        pl.semaphore_signal(
-            barrier, inc=1, device_id=chip(spot, plane + 1), device_id_type=MESH
-        )
-
-    k_all = k_ref[...]
-    v_all = v_ref[...]
-    kv_stage[0] = jnp.where(low, k_all[:, wide:], k_all[:, :wide])
-    kv_stage[1] = jnp.where(low, v_all[:, wide:], v_all[:, :wide])
-    kv[own, 0, pl.ds(mine, rows), :] = jnp.where(low, k_all[:, :wide], k_all[:, wide:])
-    kv[own, 1, pl.ds(mine, rows), :] = jnp.where(low, v_all[:, :wide], v_all[:, wide:])
-    for stage, held, ref in ((q_stage, qs, q_ref), (g_stage, gs, g_ref)):
+        for part_of in range(2):
+            for which in range(2):
+                z_copy(which, part_of).start()
+
+    for delta in range(1, window):
+
+        @pl.when(spot + delta < window)
+        def _(delta=delta):
+            for which in range(2):
+                plane_copy(delta, which).start()
+
+    swaps = []
+    for index, (stage, held, ref) in enumerate(
+        ((q_stage, qs, q_ref), (g_stage, gs, g_ref))
+    ):
         for head in range(HALF_Q):
             left = ref[:, head * HD : (head + 1) * HD]
             right = ref[:, (head + HALF_Q) * HD : (head + HALF_Q + 1) * HD]
             stage[head] = jnp.where(low, right, left)
             held[head, pl.ds(mine, rows), :] = jnp.where(low, left, right)
-
-    neighbours = has_prev.astype(jnp.int32) + has_next.astype(jnp.int32)
-    pl.semaphore_wait(barrier, window + neighbours)
-
-    kv_swap = remote(
-        kv_stage,
-        kv.at[own, :, pl.ds(mine, rows), :],
-        ex_send.at[0],
-        ex_recv.at[0],
-        partner,
-    )
-    q_swap = remote(
-        q_stage, qs.at[:, pl.ds(mine, rows), :], ex_send.at[1], ex_recv.at[1], partner
-    )
-    g_swap = remote(
-        g_stage, gs.at[:, pl.ds(mine, rows), :], ex_send.at[2], ex_recv.at[2], partner
-    )
-    kv_swap.start()
-    q_swap.start()
-    kv_swap.wait_recv()
-
-    z_send_copy = remote(
-        kv.at[own], kv.at[spot], z_sems.at[0], z_sems.at[1], chip(spot, plane + 1)
-    )
-    z_recv_copy = remote(
-        kv.at[own], kv.at[spot], z_sems.at[0], z_sems.at[1], partner
-    )
-
-    @pl.when(has_next)
-    def _():
-        z_send_copy.start()
-
-    def plane_copy(delta, source):
-        return remote(
-            source,
-            kv.at[spot],
-            plane_send.at[delta],
-            plane_recv.at[spot],
-            chip((spot + delta) % window, plane),
-        )
-
-    for delta in range(1, window):
-
-        @pl.when(spot + delta < window)
-        def _(delta=delta):
-            plane_copy(delta, kv.at[own]).start()
-
-    g_swap.start()
+        swap = remote(
+            stage,
+            held.at[:, pl.ds(mine, rows), :],
+            ex_send.at[index + 1],
+            ex_recv.at[index + 1],
+            partner,
+        )
+        swap.start()
+        swaps.append(swap)
+    q_swap, g_swap = swaps
 
     ends = []
     total = jnp.int32(0)
@@ -254,31 +282,46 @@
     for head in range(HALF_Q):
         kv_head, lanes = head_lanes(head)
         q_turned[kv_head, :, lanes] = qs[head].T
+    kv_swap.wait_recv()
     absorb(own, pair, True)
 
     @pl.when(has_prev)
     def _():
-        z_recv_copy.wait_recv()
-        for delta in range(1, window):
-
-            @pl.when(spot + delta >= window)
-            def _(delta=delta):
-                plane_copy(delta, kv.at[spot]).start()
+        for part_of in range(2):
+            for row_core in range(2):
+                z_arrival(row_core, part_of).wait_recv()
+            for delta in range(1, window):
+
+                @pl.when(spot + delta >= window)
+                def _(delta=delta, part_of=part_of):
+                    plane_pass(delta, part_of).start()
 
     def forward_step(turn, carried):
         slot = jnp.where(turn < spot, spot - 1 - turn, turn)
 
         @pl.when((slot < spot) | has_prev)
         def _():
-            @pl.when(slot != spot)
+            @pl.when(slot < spot)
             def _():
-                remote(
-                    kv.at[own],
-                    kv.at[slot],
-                    plane_send.at[0],
-                    plane_recv.at[slot],
-                    partner,
-                ).wait_recv()
+                for row_core in range(2):
+                    remote(
+                        kv_stage.at[0],
+                        kv.at[slot, :, pl.ds(row_core * rows, rows), :],
+                        plane_send.at[0, row_core],
+                        plane_recv.at[slot, row_core],
+                        partner,
+                    ).wait_recv()
+
+            @pl.when(slot > spot)
+            def _():
+                for part_of in range(2):
+                    remote(
+                        kv.at[own, part_of],
+                        kv.at[slot, part_of],
+                        plane_send.at[0, part_of],
+                        plane_recv.at[slot, part_of],
+                        partner,
+                    ).wait_recv()
 
             block = jnp.where(slot < spot, plane, plane - 1) * window + slot
             absorb(slot, block, False)
@@ -337,13 +380,22 @@
                 kv[slot, 0, :, columns].T, ds_buf[kv_head]
             )
 
-    def part_copy(slot):
+    def part_copy(slot, row_core):
         return remote(
-            part.at[slot],
-            part_in.at[spot],
-            part_send.at[slot],
-            part_recv.at[spot],
-            chip(slot, plane),
+            part.at[slot, :, pl.ds(row_core * rows, rows), :],
+            part_in.at[spot, core],
+            part_send.at[slot, row_core],
+            part_recv.at[spot, core],
+            at_chip(slot, plane, row_core),
+        )
+
+    def part_swap():
+        return remote(
+            part.at[spot, :, pl.ds(theirs, rows), :],
+            part_in.at[spot, core],
+            part_send.at[spot, 0],
+            part_recv.at[spot, core],
+            partner,
         )
 
     def backward_step(turn, carried):
@@ -358,37 +410,52 @@
 
             @pl.when(slot != spot)
             def _():
-                part_copy(slot).start()
+                for row_core in range(2):
+                    part_copy(slot, row_core).start()
+
+            @pl.when(slot == spot)
+            def _():
+                part_swap().start()
 
         return carried
 
     lax.fori_loop(0, window, backward_step, 0)
 
-    def part_arrived(slot):
+    def part_arrived(slot, which):
         remote(
-            part.at[slot], part_in.at[slot], part_send.at[slot], part_recv.at[slot], partner
+            part.at[slot, :, pl.ds(0, rows), :],
+            part_in.at[slot, which],
+            part_send.at[slot, 0],
+            part_recv.at[slot, which],
+            partner,
         ).wait_recv()
 
-    z_back = remote(z_out, z_in, z_sems.at[2], z_sems.at[3], chip(spot, plane - 1))
-    z_back_in = remote(z_out, z_in, z_sems.at[2], z_sems.at[3], partner)
+    z_back = remote(z_out, z_in, z_back_sems.at[0], z_back_sems.at[1], at_chip(spot, plane - 1, core))
+    z_back_in = remote(z_out, z_in, z_back_sems.at[0], z_back_sems.at[1], partner)
+
+    def gather(slot, carried):
+        for which in range(2):
+            part_arrived(slot, which)
+            totals[which] += part_in[slot, which].astype(F32)
+        return carried
 
     @pl.when(has_prev)
     def _():
-        own_part[...] = part[spot].astype(F32)
-
-        def gather(slot, carried):
-            part_arrived(slot)
-            own_part[...] += part_in[slot].astype(F32)
-            return carried
-
+        part_arrived(spot, 1 - core)
+        totals[core] = part[spot, :, pl.ds(mine, rows), :].astype(F32)
+        totals[1 - core] = part_in[spot, 1 - core].astype(F32)
         lax.fori_loop(0, spot, gather, 0)
-        z_out[...] = own_part[...].astype(BF16)
+        z_out[...] = totals[...].astype(BF16)
         z_back.start()
 
     def put_own(which, columns, value):
         own_part[which, :, columns] = value
 
     contribute(own, put_own)
+
+    f_out[...] = own_part[:, pl.ds(theirs, rows), :].astype(BF16)
+    f_swap = remote(f_out, f_in, fin_send.at[2], fin_recv.at[2], partner)
+    f_swap.start()
 
     for head in range(HALF_Q):
         kv_head, lanes = head_lanes(head)
@@ -402,12 +469,10 @@
     )
     dq_swap.start()
 
-    def gather_own(slot, carried):
-        part_arrived(slot)
-        own_part[...] += part_in[slot].astype(F32)
-        return carried
-
-    lax.fori_loop(spot + 1, window, gather_own, 0)
+    totals[core] = own_part[:, pl.ds(mine, rows), :]
+    f_swap.wait_recv()
+    totals[1 - core] = f_in[...].astype(F32)
+    lax.fori_loop(spot + 1, window, gather, 0)
 
     o_swap.wait_recv()
     dq_swap.wait_recv()
@@ -423,39 +488,44 @@
     @pl.when(has_next)
     def _():
         z_back_in.wait_recv()
-        own_part[...] += z_in[...].astype(F32)
-
-    f_out[...] = own_part[:, pl.ds(theirs, rows), :].astype(BF16)
-    f_swap = remote(f_out, f_in, fin_send.at[2], fin_recv.at[2], partner)
-    f_swap.start()
-    f_swap.wait_recv()
-    for which, ref in ((0, dk_ref), (1, dv_ref)):
-        here = own_part[which, pl.ds(mine, rows), :].astype(BF16)
-        there = f_in[which]
-        ref[:, :wide] = jnp.where(low, here, there)
-        ref[:, wide:] = jnp.where(low, there, here)
+        totals[...] += z_in[...].astype(F32)
+
+    for which in range(2):
+        half = slice(which * wide, (which + 1) * wide)
+        dk_ref[:, half] = totals[which, 0].astype(BF16)
+        dv_ref[:, half] = totals[which, 1].astype(BF16)
 
     for copy in (kv_swap, q_swap, g_swap, o_swap, dq_swap, f_swap):
         copy.wait_send()
 
     @pl.when(has_next)
     def _():
-        z_send_copy.wait_send()
+        for part_of in range(2):
+            for which in range(2):
+                z_copy(which, part_of).wait_send()
 
     @pl.when(has_prev)
     def _():
         z_back.wait_send()
+        part_swap().wait_send()
 
     for delta in range(1, window):
 
-        @pl.when((spot + delta < window) | has_prev)
+        @pl.when(spot + delta < window)
         def _(delta=delta):
-            plane_copy(delta, kv.at[own]).wait_send()
+            for which in range(2):
+                plane_copy(delta, which).wait_send()
+
+        @pl.when((spot + delta >= window) & has_prev)
+        def _(delta=delta):
+            for part_of in range(2):
+                plane_pass(delta, part_of).wait_send()
 
     def sent(slot, carried):
         @pl.when(((slot < spot) | has_prev) & (slot != spot))
         def _():
-            part_copy(slot).wait_send()
+            for row_core in range(2):
+                part_copy(slot, row_core).wait_send()
 
         return carried
 
@@ -463,8 +533,20 @@
 
 
 def hand_over(*refs):
-    for source, target in zip(refs[:4], refs[4:]):
-        target[...] = source[...]
+    sems = refs[8]
+    copies = []
+    for source, target in zip(refs[:4], refs[4:8]):
+        rows = source.shape[0]
+        step = rows // 2
+        for first in range(0, rows, step):
+            piece = pl.ds(first, step)
+            copy = pltpu.make_async_copy(
+                source.at[piece, :], target.at[piece, :], sems.at[len(copies)]
+            )
+            copy.start()
+            copies.append(copy)
+    for copy in copies:
+        copy.wait()
 
 
 def per_device(seq, tp, query_rows, key_rows, value_rows, out_grad, doc_lengths):
@@ -484,7 +566,7 @@
         vmem((HALF_Q, pair_rows, HD), BF16),
         vmem((HALF_Q, rows, HD), BF16),
         vmem((HALF_Q, rows, HD), BF16),
-        vmem((2, rows, wide), BF16),
+        vmem((2, 2, rows, wide), BF16),
         vmem((blocks, HALF_KV, pair_rows, long), BF16),
         vmem((blocks, HALF_KV, 1, long), F32),
         vmem((HALF_KV, 1, long), F32),
@@ -500,10 +582,11 @@
         vmem((HALF_KV, pair_rows, long), BF16),
         vmem((HALF_KV, pair_rows, long), BF16),
         vmem((window, 2, pair_rows, wide), BF16),
-        vmem((window, 2, pair_rows, wide), BF16),
+        vmem((window, 2, 2, rows, wide), BF16),
         vmem((2, pair_rows, wide), F32),
-        vmem((2, pair_rows, wide), BF16),
-        vmem((2, pair_rows, wide), BF16),
+        vmem((2, 2, rows, wide), F32),
+        vmem((2, 2, rows, wide), BF16),
+        vmem((2, 2, rows, wide), BF16),
         vmem((HALF_Q, pair_rows, HD), BF16),
         vmem((HALF_Q, rows, HD), BF16),
         vmem((HALF_Q, pair_rows, HD), BF16),
@@ -512,11 +595,13 @@
         vmem((2, rows, wide), BF16),
         dma((3,)),
         dma((3,)),
-        dma((4,)),
-        dma((window,)),
-        dma((window,)),
-        dma((window,)),
-        dma((window,)),
+        dma((2, 2)),
+        dma((2, 2)),
+        dma((2,)),
+        dma((window, 2)),
+        dma((window, 2)),
+        dma((window, 2)),
+        dma((window, 2)),
         dma((3,)),
         dma((3,)),
     ]
@@ -542,11 +627,13 @@
         ),
         name="packed_attention",
     )(query_rows, key_rows, value_rows, out_grad, doc_lengths)
+    left = pl.BlockSpec(memory_space=pl.ANY)
     return pl.pallas_call(
         hand_over,
         out_shape=shapes,
-        in_specs=[whole] * 4,
-        out_specs=(whole,) * 4,
+        in_specs=[left] * 4,
+        out_specs=(left,) * 4,
+        scratch_shapes=[dma((8,))],
         name="hand_over",
     )(*results)
 

time: 58 us -> 96.7 us (1.67)
  Pallas kernels: 57.2 us -> 95.9 us
    pallas_call x1, Pallas kernels: 2.51 us -> 48.8 us  [per_device(): pl.pallas_call(hand_over, out_shape=shapes, in_specs=[left] * 4, out_spec...]
    pallas_call x1, Pallas kernels: 54.7 us -> 47 us  [per_device(): pl.pallas_call(body, out_shape=shapes, in_specs=[whole] * 4 + [pl.BlockSp...]
where the time goes in v3:
time: 96.7 us; the launch traced here: 96.5 us
  Pallas kernels  95.9 us (99%)
    pallas_call x1, Pallas kernels, per_device(): pl.pallas_call(hand_over, out_shape=shapes, in_specs=[left] * 4, out_spec...  48.8 us
    pallas_call x1, Pallas kernels, per_device(): pl.pallas_call(body, out_shape=shapes, in_specs=[whole] * 4 + [pl.BlockSp...  47 us

profile of v3, /device:TPU:13, one launch (start us, length us, event | category | flops | bytes accessed | tf_op | source)
XLA Modules:
  0.0 96.5 jit_solution(18312160587351039041)
XLA Ops:
  0.6 47.0 %packed_attention.1 = (bf16[128,2560]{1,0:T(8,128)(2,1)}, bf16[128,2560]{1,0:T(8,128)(2,1)}, bf16[128,512]{1,0:T(8,128)(2,1)}, bf16[128,512]{1,0:T(8,128)(2,1)}) custom-call(bf16[128,2560]{1,0:T(8,128)(2,1)} %refs_0_.1, bf16[128,512]{1,0:T(8,128)(2,1)} %refs_1_.1, bf16[128,512]{1,0:T(8,128)(2,1)} %refs_2_.1, bf16[128,2560]{1,0:T(8,128)(2,1)} %refs_3_.1, ...), custom_call_target="tpu_custom_call" | custom-call | tf_op jit(solution)/shard_map/packed_attention/pallas_call | solution.py:617
  47.7 48.8 %hand_over.1 = (bf16[128,2560]{1,0:T(8,128)(2,1)}, bf16[128,2560]{1,0:T(8,128)(2,1)}, bf16[128,512]{1,0:T(8,128)(2,1)}, bf16[128,512]{1,0:T(8,128)(2,1)}) custom-call(bf16[128,2560]{1,0:T(8,128)(2,1)} %get-tuple-element.8.refs_0_, bf16[128,2560]{1,0:T(8,128)(2,1)} %get-tuple-element.9.refs_1_, bf16[128,512]{1,0:T(8,128)(2,1)} %get-tuple-element.10.refs_2_, ...), custom_call_target="tpu_custom_call" | custom-call | tf_op jit(solution)/shard_map/hand_over/pallas_call | solution.py:631

commit v4 on v3

--- a/solution.py
+++ b/solution.py
@@ -297,7 +297,7 @@
                     plane_pass(delta, part_of).start()
 
     def forward_step(turn, carried):
-        slot = jnp.where(turn < spot, spot - 1 - turn, turn)
+        slot = (spot + window - turn) % window
 
         @pl.when((slot < spot) | has_prev)
         def _():
@@ -399,7 +399,7 @@
         )
 
     def backward_step(turn, carried):
-        slot = window - 1 - turn
+        slot = (spot + window - 1 - turn) % window
 
         @pl.when((slot < spot) | has_prev)
         def _():
@@ -533,19 +533,28 @@
 
 
 def hand_over(*refs):
-    sems = refs[8]
-    copies = []
-    for source, target in zip(refs[:4], refs[4:8]):
+    sources, targets, holds, sems = refs[:4], refs[4:8], refs[8:12], refs[12]
+    pieces = []
+    for index, source in enumerate(sources):
         rows = source.shape[0]
-        step = rows // 2
-        for first in range(0, rows, step):
-            piece = pl.ds(first, step)
-            copy = pltpu.make_async_copy(
-                source.at[piece, :], target.at[piece, :], sems.at[len(copies)]
-            )
-            copy.start()
-            copies.append(copy)
-    for copy in copies:
+        cuts = 2 if source.shape[1] > rows * 8 else 1
+        for first in range(0, rows, rows // cuts):
+            pieces.append((index, pl.ds(first, rows // cuts)))
+    inward, outward = [], []
+    for at, (index, piece) in enumerate(pieces):
+        copy = pltpu.make_async_copy(
+            sources[index].at[piece, :], holds[index].at[piece, :], sems.at[0, at]
+        )
+        copy.start()
+        inward.append(copy)
+    for at, (index, piece) in enumerate(pieces):
+        inward[at].wait()
+        copy = pltpu.make_async_copy(
+            holds[index].at[piece, :], targets[index].at[piece, :], sems.at[1, at]
+        )
+        copy.start()
+        outward.append(copy)
+    for copy in outward:
         copy.wait()
 
 
@@ -633,7 +642,7 @@
         out_shape=shapes,
         in_specs=[left] * 4,
         out_specs=(left,) * 4,
-        scratch_shapes=[dma((8,))],
+        scratch_shapes=[vmem(x.shape, BF16) for x in shapes] + [dma((2, 8))],
         name="hand_over",
     )(*results)
 

time: 96.7 us -> 50 us (0.52)
  Pallas kernels: 95.9 us -> 49.2 us
    pallas_call x1, Pallas kernels: 48.8 us -> 2.24 us  [per_device(): pl.pallas_call(hand_over, out_shape=shapes, in_specs=[left] * 4, out_spec...]
where the time goes in v4:
time: 50 us; the launch traced here: 49.9 us
  Pallas kernels  49.2 us (98%)
  between operations  0.64 us (1%)
    pallas_call x1, Pallas kernels, per_device(): pl.pallas_call(body, out_shape=shapes, in_specs=[whole] * 4 + [pl.BlockSp...  47 us
    pallas_call x1, Pallas kernels, per_device(): pl.pallas_call(hand_over, out_shape=shapes, in_specs=[left] * 4, out_spec...  2.24 us

profile of v4, /device:TPU:13, one launch (start us, length us, event | category | flops | bytes accessed | tf_op | source)
XLA Modules:
  0.0 49.9 jit_solution(3127591523558173738)
XLA Ops:
  0.6 47.0 %packed_attention.1 = (bf16[128,2560]{1,0:T(8,128)(2,1)}, bf16[128,2560]{1,0:T(8,128)(2,1)}, bf16[128,512]{1,0:T(8,128)(2,1)}, bf16[128,512]{1,0:T(8,128)(2,1)}) custom-call(bf16[128,2560]{1,0:T(8,128)(2,1)} %refs_0_.1, bf16[128,512]{1,0:T(8,128)(2,1)} %refs_1_.1, bf16[128,512]{1,0:T(8,128)(2,1)} %refs_2_.1, bf16[128,2560]{1,0:T(8,128)(2,1)} %refs_3_.1, ...), custom_call_target="tpu_custom_call" | custom-call | tf_op jit(solution)/shard_map/packed_attention/pallas_call | solution.py:626
  47.6 2.2 %hand_over.1 = (bf16[128,2560]{1,0:T(8,128)(2,1)}, bf16[128,2560]{1,0:T(8,128)(2,1)}, bf16[128,512]{1,0:T(8,128)(2,1)}, bf16[128,512]{1,0:T(8,128)(2,1)}) custom-call(bf16[128,2560]{1,0:T(8,128)(2,1)} %get-tuple-element.8.refs_0_, bf16[128,2560]{1,0:T(8,128)(2,1)} %get-tuple-element.9.refs_1_, bf16[128,512]{1,0:T(8,128)(2,1)} %get-tuple-element.10.refs_2_, ...), custom_call_target="tpu_custom_call" | custom-call | tf_op jit(solution)/shard_map/hand_over/pallas_call | solution.py:640

commit v5 on v4

--- a/solution.py
+++ b/solution.py
@@ -380,26 +380,31 @@
                 kv[slot, 0, :, columns].T, ds_buf[kv_head]
             )
 
-    def part_copy(slot, row_core):
-        return remote(
-            part.at[slot, :, pl.ds(row_core * rows, rows), :],
-            part_in.at[spot, core],
-            part_send.at[slot, row_core],
-            part_recv.at[spot, core],
+    def part_copy(slot, row_core, part_of):
+        return remote(
+            part.at[slot, part_of, pl.ds(row_core * rows, rows), :],
+            part_in.at[spot, core, part_of],
+            part_send.at[slot, row_core, part_of],
+            part_recv.at[spot, core, part_of],
             at_chip(slot, plane, row_core),
         )
 
-    def part_swap():
-        return remote(
-            part.at[spot, :, pl.ds(theirs, rows), :],
-            part_in.at[spot, core],
-            part_send.at[spot, 0],
-            part_recv.at[spot, core],
+    def part_swap(part_of):
+        return remote(
+            part.at[spot, part_of, pl.ds(theirs, rows), :],
+            part_in.at[spot, core, part_of],
+            part_send.at[spot, 0, part_of],
+            part_recv.at[spot, core, part_of],
             partner,
         )
 
     def backward_step(turn, carried):
-        slot = (spot + window - 1 - turn) % window
+        pattern = window - 1 - turn
+        slot = 0
+        bit = 1
+        while bit < window:
+            slot = slot + ((spot // bit + pattern // bit) % 2) * bit
+            bit *= 2
 
         @pl.when((slot < spot) | has_prev)
         def _():
@@ -410,43 +415,64 @@
 
             @pl.when(slot != spot)
             def _():
-                for row_core in range(2):
-                    part_copy(slot, row_core).start()
+                for part_of in range(2):
+                    for row_core in range(2):
+                        part_copy(slot, row_core, part_of).start()
 
             @pl.when(slot == spot)
             def _():
-                part_swap().start()
+                for part_of in range(2):
+                    part_swap(part_of).start()
 
         return carried
 
     lax.fori_loop(0, window, backward_step, 0)
 
-    def part_arrived(slot, which):
+    def part_arrived(slot, which, part_of):
         remote(
-            part.at[slot, :, pl.ds(0, rows), :],
-            part_in.at[slot, which],
-            part_send.at[slot, 0],
-            part_recv.at[slot, which],
+            part.at[slot, part_of, pl.ds(0, rows), :],
+            part_in.at[slot, which, part_of],
+            part_send.at[slot, 0, part_of],
+            part_recv.at[slot, which, part_of],
             partner,
         ).wait_recv()
 
-    z_back = remote(z_out, z_in, z_back_sems.at[0], z_back_sems.at[1], at_chip(spot, plane - 1, core))
-    z_back_in = remote(z_out, z_in, z_back_sems.at[0], z_back_sems.at[1], partner)
-
-    def gather(slot, carried):
-        for which in range(2):
-            part_arrived(slot, which)
-            totals[which] += part_in[slot, which].astype(F32)
-        return carried
+    def z_back(part_of):
+        return remote(
+            z_out.at[part_of],
+            z_in.at[part_of],
+            z_back_sems.at[0, part_of],
+            z_back_sems.at[1, part_of],
+            at_chip(spot, plane - 1, core),
+        )
+
+    def z_back_in(part_of):
+        return remote(
+            z_out.at[part_of],
+            z_in.at[part_of],
+            z_back_sems.at[0, part_of],
+            z_back_sems.at[1, part_of],
+            partner,
+        )
+
+    def gather(part_of):
+        def step(slot, carried):
+            for which in range(2):
+                part_arrived(slot, which, part_of)
+                totals[part_of, which] += part_in[slot, which, part_of].astype(F32)
+            return carried
+
+        return step
 
     @pl.when(has_prev)
     def _():
-        part_arrived(spot, 1 - core)
-        totals[core] = part[spot, :, pl.ds(mine, rows), :].astype(F32)
-        totals[1 - core] = part_in[spot, 1 - core].astype(F32)
-        lax.fori_loop(0, spot, gather, 0)
-        z_out[...] = totals[...].astype(BF16)
-        z_back.start()
+        for part_of in range(2):
+            part_arrived(spot, 1 - core, part_of)
+            totals[part_of, core] = part[spot, part_of, pl.ds(mine, rows), :].astype(F32)
+            totals[part_of, 1 - core] = part_in[spot, 1 - core, part_of].astype(F32)
+            lax.fori_loop(0, spot, gather(part_of), 0)
+            z_out[part_of] = totals[part_of].astype(BF16)
+            z_back(part_of).start()
 
     def put_own(which, columns, value):
         own_part[which, :, columns] = value
@@ -469,10 +495,11 @@
     )
     dq_swap.start()
 
-    totals[core] = own_part[:, pl.ds(mine, rows), :]
     f_swap.wait_recv()
-    totals[1 - core] = f_in[...].astype(F32)
-    lax.fori_loop(spot + 1, window, gather, 0)
+    for part_of in range(2):
+        totals[part_of, core] = own_part[part_of, pl.ds(mine, rows), :]
+        totals[part_of, 1 - core] = f_in[part_of].astype(F32)
+        lax.fori_loop(spot + 1, window, gather(part_of), 0)
 
     o_swap.wait_recv()
     dq_swap.wait_recv()
@@ -487,13 +514,14 @@
 
     @pl.when(has_next)
     def _():
-        z_back_in.wait_recv()
+        for part_of in range(2):
+            z_back_in(part_of).wait_recv()
         totals[...] += z_in[...].astype(F32)
 
     for which in range(2):
         half = slice(which * wide, (which + 1) * wide)
-        dk_ref[:, half] = totals[which, 0].astype(BF16)
-        dv_ref[:, half] = totals[which, 1].astype(BF16)
+        dk_ref[:, half] = totals[0, which].astype(BF16)
+        dv_ref[:, half] = totals[1, which].astype(BF16)
 
     for copy in (kv_swap, q_swap, g_swap, o_swap, dq_swap, f_swap):
         copy.wait_send()
@@ -506,8 +534,9 @@
 
     @pl.when(has_prev)
     def _():
-        z_back.wait_send()
-        part_swap().wait_send()
+        for part_of in range(2):
+            z_back(part_of).wait_send()
+            part_swap(part_of).wait_send()
 
     for delta in range(1, window):
 
@@ -524,8 +553,9 @@
     def sent(slot, carried):
         @pl.when(((slot < spot) | has_prev) & (slot != spot))
         def _():
-            for row_core in range(2):
-                part_copy(slot, row_core).wait_send()
+            for part_of in range(2):
+                for row_core in range(2):
+                    part_copy(slot, row_core, part_of).wait_send()
 
         return carried
 
@@ -606,11 +636,11 @@
         dma((3,)),
         dma((2, 2)),
         dma((2, 2)),
-        dma((2,)),
+        dma((2, 2)),
         dma((window, 2)),
         dma((window, 2)),
-        dma((window, 2)),
-        dma((window, 2)),
+        dma((window, 2, 2)),
+        dma((window, 2, 2)),
         dma((3,)),
         dma((3,)),
     ]

time: 50 us -> 48.7 us (0.974)
  Pallas kernels: 49.2 us -> 47.8 us
    pallas_call x1, Pallas kernels: 47 us -> 45.6 us  [per_device(): pl.pallas_call(body, out_shape=shapes, in_specs=[whole] * 4 + [pl.BlockSp...]
where the time goes in v5:
time: 48.7 us; the launch traced here: 48.5 us
  Pallas kernels  47.8 us (98%)
  between operations  0.64 us (1%)
    pallas_call x1, Pallas kernels, per_device(): pl.pallas_call(body, out_shape=shapes, in_specs=[whole] * 4 + [pl.BlockSp...  45.6 us
    pallas_call x1, Pallas kernels, per_device(): pl.pallas_call(hand_over, out_shape=shapes, in_specs=[left] * 4, out_spec...  2.24 us

profile of v5, /device:TPU:13, one launch (start us, length us, event | category | flops | bytes accessed | tf_op | source)
XLA Modules:
  0.0 48.5 jit_solution(15398577410381668386)
XLA Ops:
  0.6 45.6 %packed_attention.1 = (bf16[128,2560]{1,0:T(8,128)(2,1)}, bf16[128,2560]{1,0:T(8,128)(2,1)}, bf16[128,512]{1,0:T(8,128)(2,1)}, bf16[128,512]{1,0:T(8,128)(2,1)}) custom-call(bf16[128,2560]{1,0:T(8,128)(2,1)} %refs_0_.1, bf16[128,512]{1,0:T(8,128)(2,1)} %refs_1_.1, bf16[128,512]{1,0:T(8,128)(2,1)} %refs_2_.1, bf16[128,2560]{1,0:T(8,128)(2,1)} %refs_3_.1, ...), custom_call_target="tpu_custom_call" | custom-call | tf_op jit(solution)/shard_map/packed_attention/pallas_call | solution.py:656
  46.2 2.2 %hand_over.1 = (bf16[128,2560]{1,0:T(8,128)(2,1)}, bf16[128,2560]{1,0:T(8,128)(2,1)}, bf16[128,512]{1,0:T(8,128)(2,1)}, bf16[128,512]{1,0:T(8,128)(2,1)}) custom-call(bf16[128,2560]{1,0:T(8,128)(2,1)} %get-tuple-element.8.refs_0_, bf16[128,2560]{1,0:T(8,128)(2,1)} %get-tuple-element.9.refs_1_, bf16[128,512]{1,0:T(8,128)(2,1)} %get-tuple-element.10.refs_2_, ...), custom_call_target="tpu_custom_call" | custom-call | tf_op jit(solution)/shard_map/hand_over/pallas_call | solution.py:670

commit v6 on v5

--- a/solution.py
+++ b/solution.py
@@ -31,13 +31,13 @@
     tp,
     window,
     planes,
-    q_ref,
+    q_hbm,
     k_ref,
     v_ref,
-    g_ref,
+    g_hbm,
     len_ref,
-    o_ref,
-    dq_ref,
+    o_hbm,
+    dq_hbm,
     dk_ref,
     dv_ref,
     kv,
@@ -83,7 +83,16 @@
     part_recv,
     fin_send,
     fin_recv,
+    q_ref,
+    g_ref,
+    o_ref,
+    dq_ref,
+    local_sems,
 ):
+    q_fetch = pltpu.make_async_copy(q_hbm, q_ref, local_sems.at[0])
+    g_fetch = pltpu.make_async_copy(g_hbm, g_ref, local_sems.at[1])
+    q_fetch.start()
+    g_fetch.start()
     rows = q_ref.shape[0]
     pair_rows = 2 * rows
     wide = HALF_KV * HD
@@ -210,9 +219,10 @@
                 plane_copy(delta, which).start()
 
     swaps = []
-    for index, (stage, held, ref) in enumerate(
-        ((q_stage, qs, q_ref), (g_stage, gs, g_ref))
+    for index, (stage, held, ref, fetch) in enumerate(
+        ((q_stage, qs, q_ref, q_fetch), (g_stage, gs, g_ref, g_fetch))
     ):
+        fetch.wait()
         for head in range(HALF_Q):
             left = ref[:, head * HD : (head + 1) * HD]
             right = ref[:, (head + HALF_Q) * HD : (head + HALF_Q + 1) * HD]
@@ -351,11 +361,11 @@
     )
     o_swap.start()
 
-    def contribute(slot, put):
-        for kv_head in range(HALF_KV):
+    def contribute(slot, put, kv_heads=tuple(range(HALF_KV))):
+        for kv_head in kv_heads:
             columns = slice(kv_head * HD, (kv_head + 1) * HD)
             wide_buf[kv_head] = dot_nn(kv[slot, 1, :, columns], g_turned[kv_head])
-        for kv_head in range(HALF_KV):
+        for kv_head in kv_heads:
             columns = slice(kv_head * HD, (kv_head + 1) * HD)
             heads = slice(kv_head * GROUP, (kv_head + 1) * GROUP)
             stacked = (GROUP * pair_rows, HD)
@@ -464,6 +474,11 @@
 
         return step
 
+    def put_own(which, columns, value):
+        own_part[which, :, columns] = value
+
+    contribute(own, put_own, (0,))
+
     @pl.when(has_prev)
     def _():
         for part_of in range(2):
@@ -474,10 +489,7 @@
             z_out[part_of] = totals[part_of].astype(BF16)
             z_back(part_of).start()
 
-    def put_own(which, columns, value):
-        own_part[which, :, columns] = value
-
-    contribute(own, put_own)
+    contribute(own, put_own, (1,))
 
     f_out[...] = own_part[:, pl.ds(theirs, rows), :].astype(BF16)
     f_swap = remote(f_out, f_in, fin_send.at[2], fin_recv.at[2], partner)
@@ -503,7 +515,11 @@
 
     o_swap.wait_recv()
     dq_swap.wait_recv()
-    for ref, everything, arrived in ((o_ref, o_all, o_in), (dq_ref, dq_all, dq_in)):
+    writes = []
+    for ref, everything, arrived, target in (
+        (o_ref, o_all, o_in, o_hbm),
+        (dq_ref, dq_all, dq_in, dq_hbm),
+    ):
         for head in range(HALF_Q):
             here = everything[head, pl.ds(mine, rows), :]
             there = arrived[head]
@@ -511,6 +527,9 @@
             ref[:, (head + HALF_Q) * HD : (head + HALF_Q + 1) * HD] = jnp.where(
                 low, there, here
             )
+        write = pltpu.make_async_copy(ref, target, local_sems.at[2 + len(writes)])
+        write.start()
+        writes.append(write)
 
     @pl.when(has_next)
     def _():
@@ -523,6 +542,8 @@
         dk_ref[:, half] = totals[0, which].astype(BF16)
         dv_ref[:, half] = totals[1, which].astype(BF16)
 
+    for write in writes:
+        write.wait()
     for copy in (kv_swap, q_swap, g_swap, o_swap, dq_swap, f_swap):
         copy.wait_send()
 
@@ -643,8 +664,14 @@
         dma((window, 2, 2)),
         dma((3,)),
         dma((3,)),
+        vmem((rows, QH * HD), BF16),
+        vmem((rows, QH * HD), BF16),
+        vmem((rows, QH * HD), BF16),
+        vmem((rows, QH * HD), BF16),
+        dma((4,)),
     ]
     whole = pl.BlockSpec(memory_space=pltpu.VMEM)
+    left = pl.BlockSpec(memory_space=pl.ANY)
 
     def body(*refs):
         kernel(tp, window, planes, *refs)
@@ -656,8 +683,8 @@
     results = pl.pallas_call(
         body,
         out_shape=shapes,
-        in_specs=[whole] * 4 + [pl.BlockSpec(memory_space=pltpu.SMEM)],
-        out_specs=(whole,) * 4,
+        in_specs=[left, whole, whole, left, pl.BlockSpec(memory_space=pltpu.SMEM)],
+        out_specs=(left, left, whole, whole),
         scratch_shapes=scratch,
         compiler_params=pltpu.CompilerParams(
             collective_id=0,
@@ -666,7 +693,6 @@
         ),
         name="packed_attention",
     )(query_rows, key_rows, value_rows, out_grad, doc_lengths)
-    left = pl.BlockSpec(memory_space=pl.ANY)
     return pl.pallas_call(
         hand_over,
         out_shape=shapes,

time: 48.7 us -> 47.8 us (0.982)
  Pallas kernels: 47.8 us -> 47 us
    pallas_call x1, Pallas kernels: 45.6 us -> 44.8 us  [per_device(): pl.pallas_call(body, out_shape=shapes, in_specs=[left, whole, whole, left...]
where the time goes in v6:
time: 47.8 us; the launch traced here: 47.6 us
  Pallas kernels  47 us (98%)
  between operations  0.64 us (1%)
    pallas_call x1, Pallas kernels, per_device(): pl.pallas_call(body, out_shape=shapes, in_specs=[left, whole, whole, left...  44.8 us
    pallas_call x1, Pallas kernels, per_device(): pl.pallas_call(hand_over, out_shape=shapes, in_specs=[left] * 4, out_spec...  2.24 us

profile of v6, /device:TPU:13, one launch (start us, length us, event | category | flops | bytes accessed | tf_op | source)
XLA Modules:
  0.0 47.6 jit_solution(8733979299530205956)
XLA Ops:
  0.6 44.8 %packed_attention.1 = (bf16[128,2560]{1,0:T(8,128)(2,1)}, bf16[128,2560]{1,0:T(8,128)(2,1)}, bf16[128,512]{1,0:T(8,128)(2,1)}, bf16[128,512]{1,0:T(8,128)(2,1)}) custom-call(bf16[128,2560]{1,0:T(8,128)(2,1)} %refs_0_.1, bf16[128,512]{1,0:T(8,128)(2,1)} %refs_1_.1, bf16[128,512]{1,0:T(8,128)(2,1)} %refs_2_.1, bf16[128,2560]{1,0:T(8,128)(2,1)} %refs_3_.1, ...), custom_call_target="tpu_custom_call" | custom-call | tf_op jit(solution)/shard_map/packed_attention/pallas_call | solution.py:683
  45.4 2.2 %hand_over.1 = (bf16[128,2560]{1,0:T(8,128)(2,1)}, bf16[128,2560]{1,0:T(8,128)(2,1)}, bf16[128,512]{1,0:T(8,128)(2,1)}, bf16[128,512]{1,0:T(8,128)(2,1)}) custom-call(bf16[128,2560]{1,0:T(8,128)(2,1)} %get-tuple-element.8.refs_0_, bf16[128,2560]{1,0:T(8,128)(2,1)} %get-tuple-element.9.refs_1_, bf16[128,512]{1,0:T(8,128)(2,1)} %get-tuple-element.10.refs_2_, ...), custom_call_target="tpu_custom_call" | custom-call | tf_op jit(solution)/shard_map/hand_over/pallas_call | solution.py:696

commit v7 on v6

--- a/solution.py
+++ b/solution.py
@@ -477,49 +477,9 @@
     def put_own(which, columns, value):
         own_part[which, :, columns] = value
 
-    contribute(own, put_own, (0,))
-
-    @pl.when(has_prev)
-    def _():
-        for part_of in range(2):
-            part_arrived(spot, 1 - core, part_of)
-            totals[part_of, core] = part[spot, part_of, pl.ds(mine, rows), :].astype(F32)
-            totals[part_of, 1 - core] = part_in[spot, 1 - core, part_of].astype(F32)
-            lax.fori_loop(0, spot, gather(part_of), 0)
-            z_out[part_of] = totals[part_of].astype(BF16)
-            z_back(part_of).start()
-
-    contribute(own, put_own, (1,))
-
-    f_out[...] = own_part[:, pl.ds(theirs, rows), :].astype(BF16)
-    f_swap = remote(f_out, f_in, fin_send.at[2], fin_recv.at[2], partner)
-    f_swap.start()
-
-    for head in range(HALF_Q):
-        kv_head, lanes = head_lanes(head)
-        dq_all[head] = (dq_acc[kv_head, :, lanes] * scaling).T.astype(BF16)
-    dq_swap = remote(
-        dq_all.at[:, pl.ds(theirs, rows), :],
-        dq_in,
-        fin_send.at[1],
-        fin_recv.at[1],
-        partner,
-    )
-    dq_swap.start()
-
-    f_swap.wait_recv()
-    for part_of in range(2):
-        totals[part_of, core] = own_part[part_of, pl.ds(mine, rows), :]
-        totals[part_of, 1 - core] = f_in[part_of].astype(F32)
-        lax.fori_loop(spot + 1, window, gather(part_of), 0)
-
-    o_swap.wait_recv()
-    dq_swap.wait_recv()
     writes = []
-    for ref, everything, arrived, target in (
-        (o_ref, o_all, o_in, o_hbm),
-        (dq_ref, dq_all, dq_in, dq_hbm),
-    ):
+
+    def deliver(ref, everything, arrived, target):
         for head in range(HALF_Q):
             here = everything[head, pl.ds(mine, rows), :]
             there = arrived[head]
@@ -530,6 +490,51 @@
         write = pltpu.make_async_copy(ref, target, local_sems.at[2 + len(writes)])
         write.start()
         writes.append(write)
+
+    def turn_back(kv_head):
+        for head in range(kv_head * GROUP, (kv_head + 1) * GROUP):
+            lanes = head_lanes(head)[1]
+            dq_all[head] = (dq_acc[kv_head, :, lanes] * scaling).T.astype(BF16)
+
+    contribute(own, put_own, (0,))
+    turn_back(0)
+    o_swap.wait_recv()
+    deliver(o_ref, o_all, o_in, o_hbm)
+
+    @pl.when(has_prev)
+    def _():
+        for part_of in range(2):
+            part_arrived(spot, 1 - core, part_of)
+            totals[part_of, core] = part[spot, part_of, pl.ds(mine, rows), :].astype(F32)
+            totals[part_of, 1 - core] = part_in[spot, 1 - core, part_of].astype(F32)
+            lax.fori_loop(0, spot, gather(part_of), 0)
+            z_out[part_of] = totals[part_of].astype(BF16)
+            z_back(part_of).start()
+
+    contribute(own, put_own, (1,))
+
+    f_out[...] = own_part[:, pl.ds(theirs, rows), :].astype(BF16)
+    f_swap = remote(f_out, f_in, fin_send.at[2], fin_recv.at[2], partner)
+    f_swap.start()
+
+    turn_back(1)
+    dq_swap = remote(
+        dq_all.at[:, pl.ds(theirs, rows), :],
+        dq_in,
+        fin_send.at[1],
+        fin_recv.at[1],
+        partner,
+    )
+    dq_swap.start()
+
+    f_swap.wait_recv()
+    for part_of in range(2):
+        totals[part_of, core] = own_part[part_of, pl.ds(mine, rows), :]
+        totals[part_of, 1 - core] = f_in[part_of].astype(F32)
+        lax.fori_loop(spot + 1, window, gather(part_of), 0)
+
+    dq_swap.wait_recv()
+    deliver(dq_ref, dq_all, dq_in, dq_hbm)
 
     @pl.when(has_next)
     def _():

time: 47.8 us -> 47.8 us (level)
  no operation moved by 1% of the time
where the time goes in v7:
time: 47.8 us; the launch traced here: 47.6 us
  Pallas kernels  47 us (98%)
  between operations  0.64 us (1%)
    pallas_call x1, Pallas kernels, per_device(): pl.pallas_call(body, out_shape=shapes, in_specs=[left, whole, whole, left...  44.8 us
    pallas_call x1, Pallas kernels, per_device(): pl.pallas_call(hand_over, out_shape=shapes, in_specs=[left] * 4, out_spec...  2.24 us

profile of v7, /device:TPU:13, one launch (start us, length us, event | category | flops | bytes accessed | tf_op | source)
XLA Modules:
  0.0 47.6 jit_solution(4744912365632892272)
XLA Ops:
  0.6 44.8 %packed_attention.1 = (bf16[128,2560]{1,0:T(8,128)(2,1)}, bf16[128,2560]{1,0:T(8,128)(2,1)}, bf16[128,512]{1,0:T(8,128)(2,1)}, bf16[128,512]{1,0:T(8,128)(2,1)}) custom-call(bf16[128,2560]{1,0:T(8,128)(2,1)} %refs_0_.1, bf16[128,512]{1,0:T(8,128)(2,1)} %refs_1_.1, bf16[128,512]{1,0:T(8,128)(2,1)} %refs_2_.1, bf16[128,2560]{1,0:T(8,128)(2,1)} %refs_3_.1, ...), custom_call_target="tpu_custom_call" | custom-call | tf_op jit(solution)/shard_map/packed_attention/pallas_call | solution.py:688
  45.4 2.2 %hand_over.1 = (bf16[128,2560]{1,0:T(8,128)(2,1)}, bf16[128,2560]{1,0:T(8,128)(2,1)}, bf16[128,512]{1,0:T(8,128)(2,1)}, bf16[128,512]{1,0:T(8,128)(2,1)}) custom-call(bf16[128,2560]{1,0:T(8,128)(2,1)} %get-tuple-element.8.refs_0_, bf16[128,2560]{1,0:T(8,128)(2,1)} %get-tuple-element.9.refs_1_, bf16[128,512]{1,0:T(8,128)(2,1)} %get-tuple-element.10.refs_2_, ...), custom_call_target="tpu_custom_call" | custom-call | tf_op jit(solution)/shard_map/hand_over/pallas_call | solution.py:701
